TPU v7x, 512 devices: a whole 4x8x8 slice. The times are simulated.
512 devices in a mesh: wide: 64 (over z, x, core), narrow: 8 (over y).
Axes of the slice: x: 4, y: 8, z: 8, core: 2. Of those that a mesh axis runs over, the one named last changes fastest.
Arguments:
- weight: bfloat16 [8192, 53248], P('narrow', 'wide'), may hold values from -0.0625 to 0.0625
- whitening: bfloat16 [8192, 8192], P('wide', 'narrow'), as said below
- sketch: bfloat16 [53248, 256], P('wide'), may hold values from -6 to 6
Outputs:
- basis: float32 [8192, 256], P(('wide', 'narrow'))
- projected: float32 [256, 53248], P('narrow', 'wide')
Inputs may be any that keep to these rules, and one draw needn't show every extreme that they name: `whitening`: zero below the diagonal; diagonal entries between 0.7 and 1.4.
All inputs are finite; a program needn't handle non-finite values.
Results may differ from a plain program's by a relative error of at most 0.02.
Values may be sent and summed in bfloat16 or wider, within the bound.
A program may use at most 64 MiB of HBM per device.

v0:
```python
import math

import jax
import jax.numpy as jnp
from jax import lax
from jax.sharding import PartitionSpec as P

D = 8192


def on_device(weight, whitening, sketch):

    def column_sum(right_side):
        partial_image = jnp.dot(weight, right_side, preferred_element_type=jnp.float32)
        return lax.psum(partial_image, "wide").astype(jnp.bfloat16)

    def back_project(rows_here):
        own_share = lax.psum_scatter(
            jnp.einsum("ik,ir->kr", whitening, rows_here, preferred_element_type=jnp.float32),
            "wide",
            scatter_dimension=0,
            tiled=True,
        )
        return lax.all_gather(own_share.astype(jnp.bfloat16), "wide", axis=0, tiled=True)

    sketch_image = column_sum(sketch)
    whitened_part = jnp.dot(whitening, sketch_image, preferred_element_type=jnp.float32)
    whitened = lax.psum(whitened_part.astype(jnp.bfloat16), "narrow")
    back_image = back_project(whitened)
    feature_part = jnp.einsum("kf,kr->fr", weight, back_image, preferred_element_type=jnp.float32)
    feature_image = lax.psum(feature_part.astype(jnp.bfloat16), "narrow")
    second_image = column_sum(feature_image)
    final_part = jnp.dot(whitening, second_image, preferred_element_type=jnp.float32)
    scale_factor = jnp.float32(math.sqrt(D))
    final_rows = lax.psum(final_part.astype(jnp.bfloat16), "narrow").astype(jnp.float32)
    local_gram = jnp.dot(final_rows.T, final_rows, precision=lax.Precision.HIGHEST)
    gram_matrix = lax.psum(local_gram, "wide")
    lower_factor = jnp.linalg.cholesky(gram_matrix)
    basis_full = jax.scipy.linalg.solve_triangular(lower_factor, final_rows.T, lower=True).T
    basis_low = basis_full.astype(jnp.bfloat16)
    row_count = basis_full.shape[0] // lax.axis_size("narrow")
    own_rows = lax.dynamic_slice_in_dim(
        basis_full, lax.axis_index("narrow") * row_count, row_count, 0
    )
    basis = own_rows * scale_factor
    weighted = back_project(basis_low)
    projected = lax.psum_scatter(
        jnp.einsum("kr,kf->rf", weighted, weight, preferred_element_type=jnp.float32).astype(
            jnp.bfloat16
        ),
        "narrow",
        scatter_dimension=0,
        tiled=True,
    ).astype(jnp.float32)
    return (basis, projected)


def solution(mesh):
    placed = (P("narrow", "wide"), P("wide", "narrow"), P("wide", None))
    return jax.shard_map(
        on_device,
        mesh=mesh,
        in_specs=placed,
        out_specs=(P(("wide", "narrow"), None), P("narrow", "wide")),
        check_vma=False,
    )
```

profile of v0, /device:TPU:1, one launch (start us, length us, event | category | flops | bytes accessed | tf_op | source)
XLA Modules:
  0.0 1449.5 jit_solution(15804912715309265440)
XLA Ops:
  7.2 1.4 copy-done
  8.6 1.8 fusion.20
  10.4 261.3 %all-reduce.15 = bf16[1024,256]{1,0:T(8,128)(2,1)S(1)} all-reduce(f32[1024,256]{1,0:T(8,128)S(1)} %fusion.20), channel_id=1, replica_groups=mesh['wide'=64,'narrow'=8] {'wide'}, use_global_device_ids=true, to_apply=%region_0.0 | all-reduce | flops 262144 | bytes 1572864 | tf_op jit(solution)/shard_map/psum | solution.py:15
  272.8 70.5 %all-reduce.8.cloned.1.call-done = bf16[128,256]{0,1:T(8,128)(2,1)} async-done(((bf16[128,256]{0,1:T(8,128)(2,1)}), bf16[128,256]{0,1:T(8,128)(2,1)}) %all-reduce.8.cloned.1.call-update) | async-done | bytes 65552 | tf_op jit(solution)/shard_map/psum | solution.py:28
  345.8 149.6 %reduce-scatter.10.cloned.1.call-done = f32[16,256]{1,0:T(8,128)} async-done(((f32[1024,256]{1,0:T(8,128)}), f32[16,256]{1,0:T(8,128)}) %reduce-scatter.10.cloned.1.call-update) | async-done | bytes 16400 | tf_op jit(solution)/shard_map/reduce_scatter | solution.py:18
  496.1 54.4 %all_gather.6 = bf16[1024,256]{1,0:T(8,128)(2,1)S(1)} all-gather(bf16[16,256]{1,0:T(8,128)(2,1)S(1)} %convert_element_type.44), channel_id=1, replica_groups=mesh['wide'=64,'narrow'=8] {'wide'}, dimensions={0}, use_global_device_ids=true | all-gather | bytes 532480 | tf_op jit(solution)/shard_map/all_gather | solution.py:24
  552.0 71.2 %all-reduce.10.cloned.1.call-done = bf16[832,256]{1,0:T(8,128)(2,1)} async-done(((bf16[832,256]{1,0:T(8,128)(2,1)}), bf16[832,256]{1,0:T(8,128)(2,1)}) %all-reduce.10.cloned.1.call-update) | async-done | bytes 426000 | tf_op jit(solution)/shard_map/psum | solution.py:31
  623.2 1.7 convolution_bitcast_fusion.1
  624.9 255.8 %all-reduce.16 = bf16[1024,256]{0,1:T(8,128)(2,1)S(1)} all-reduce(f32[1024,256]{0,1:T(8,128)S(1)} %convolution_bitcast_fusion.1), channel_id=1, replica_groups=mesh['wide'=64,'narrow'=8] {'wide'}, use_global_device_ids=true, to_apply=%region_4.0 | all-reduce | flops 262144 | bytes 1572864 | tf_op jit(solution)/shard_map/psum | solution.py:15
  881.7 71.9 %all-reduce.12.cloned.1.call-done = bf16[128,256]{0,1:T(8,128)(2,1)} async-done(((bf16[128,256]{0,1:T(8,128)(2,1)}), bf16[128,256]{0,1:T(8,128)(2,1)}) %all-reduce.12.cloned.1.call-update) | async-done | bytes 65552 | tf_op jit(solution)/shard_map/psum | solution.py:35
  953.6 1.8 fusion.21
  955.7 192.1 %all-reduce.14.cloned.1.call-done = f32[256,256]{0,1:T(8,128)} async-done(((f32[256,256]{0,1:T(8,128)}), f32[256,256]{0,1:T(8,128)}) %all-reduce.14.cloned.1.call-update) | async-done | bytes 262160 | tf_op jit(solution)/shard_map/psum | solution.py:37
  1149.9 11.7 cholesky.50
  1161.6 9.8 custom-call.15
  1171.9 11.7 cholesky.105
  1185.9 4.3 while.1
  1186.7 1.4 bitcast_dynamic-update-slice_fusion.2
  1188.7 1.4 bitcast_dynamic-update-slice_fusion.2
  1190.1 19.7 %custom-call.16 = f32[2,128,128]{1,2,0:T(8,128)S(1)} custom-call(f32[2,128,128]{2,1,0:T(8,128)S(1)} %get-tuple-element.9), custom_call_target="InvertDiagBlocksLowerTriangular" | custom-call | tf_op jit(solution)/shard_map/jit(_solve_triangular)/triangular_solve | solution.py:39
  1212.3 140.1 %reduce-scatter.12.cloned.1.call-done = f32[16,256]{1,0:T(8,128)} async-done(((f32[1024,256]{1,0:T(8,128)}), f32[16,256]{1,0:T(8,128)}) %reduce-scatter.12.cloned.1.call-update) | async-done | bytes 16400 | tf_op jit(solution)/shard_map/reduce_scatter | solution.py:18
  1353.1 54.4 %all_gather.7 = bf16[1024,256]{1,0:T(8,128)(2,1)S(1)} all-gather(bf16[16,256]{1,0:T(8,128)(2,1)S(1)} %convert_element_type.51), channel_id=1, replica_groups=mesh['wide'=64,'narrow'=8] {'wide'}, dimensions={0}, use_global_device_ids=true | all-gather | bytes 532480 | tf_op jit(solution)/shard_map/all_gather | solution.py:24
  1407.5 1.5 convolution_convert_fusion
  1409.9 31.3 %reduce-scatter.8.cloned.1.call-done = bf16[32,832]{1,0:T(8,128)(2,1)} async-done(((bf16[256,832]{1,0:T(8,128)(2,1)}), bf16[32,832]{1,0:T(8,128)(2,1)}) %reduce-scatter.8.cloned.1.call-update) | async-done | bytes 53264 | tf_op jit(solution)/shard_map/reduce_scatter | solution.py:47
  1441.2 1.5 convert_element_type.53
  (50 shorter events, 15.6 us)
Async XLA Ops:
  7.2 1.5 copy-start
  7.2 264.5 %copy-start.1 = (bf16[128,1024]{1,0:T(8,128)(2,1)S(1)}, bf16[128,1024]{1,0:T(8,128)(2,1)}, u32[]{:S(2)}) copy-start(bf16[128,1024]{1,0:T(8,128)(2,1)} %param.4) | copy-start | bytes 786436
  7.2 336.1 %all-reduce.8.cloned.1.call-start = ((), (), s32[]{:S(2)}) async-start(), calls=%async_computation.3 | async-start | bytes 131072 | tf_op jit(solution)/shard_map/psum | solution.py:28
  272.7 222.7 %reduce-scatter.10.cloned.1.call-start = ((), (), s32[]{:S(2)}) async-start(), calls=%async_computation.8 | async-start | bytes 1064960 | tf_op jit(solution)/shard_map/reduce_scatter | solution.py:18
  345.8 277.4 %all-reduce.10.cloned.1.call-start = ((), (), s32[]{:S(2)}) async-start(), calls=%async_computation.4 | async-start | bytes 851968 | tf_op jit(solution)/shard_map/psum | solution.py:31
  552.0 401.7 %all-reduce.12.cloned.1.call-start = ((), (), s32[]{:S(2)}) async-start(), calls=%async_computation.5 | async-start | bytes 131072 | tf_op jit(solution)/shard_map/psum | solution.py:35
  881.7 266.1 %all-reduce.14.cloned.1.call-start = ((), (), s32[]{:S(2)}) async-start(), calls=%async_computation.6 | async-start | bytes 524288 | tf_op jit(solution)/shard_map/psum | solution.py:37
  955.4 396.9 %reduce-scatter.12.cloned.1.call-start = ((), (), s32[]{:S(2)}) async-start(), calls=%async_computation.9 | async-start | bytes 1064960 | tf_op jit(solution)/shard_map/reduce_scatter | solution.py:18
  1148.8 61.0 %copy-start.2 = (bf16[128,256]{0,1:T(8,128)(2,1)S(1)}, bf16[128,256]{0,1:T(8,128)(2,1)}, u32[]{:S(2)}) copy-start(bf16[128,256]{0,1:T(8,128)(2,1)} %all-reduce.12.cloned.1.call-done) | copy-start | bytes 196612
  1212.2 228.9 %reduce-scatter.8.cloned.1.call-start = ((), (), s32[]{:S(2)}) async-start(), calls=%async_computation.7 | async-start | bytes 516096 | tf_op jit(solution)/shard_map/reduce_scatter | solution.py:47
Sparse Core Ops, SparseCore 0:
  272.9 70.3 all-reduce.7
  348.5 146.8 reduce-scatter.9
  552.1 71.0 all-reduce.9
  881.8 71.7 all-reduce.11
  957.3 190.3 all-reduce.13
  1212.4 139.9 reduce-scatter.11
  1409.2 31.8 reduce-scatter.7
where the time goes:
time: 1450 us
  waiting for transfers between devices  727 us (50%)
  blocking collectives  626 us (43%)
  other arithmetic  57.8 us (4%)
  between operations  15.7 us (1%)
    psum x2, blocking collectives, column_sum(): return lax.psum(partial_image, 'wide').astype(jnp.bfloat16)  517 us
    reduce_scatter x2, waiting for transfers between devices, back_project(): lax.psum_scatter(jnp.einsum('ik,ir->kr', whitening, rows_here, preferred_...  290 us
    psum x1, waiting for transfers between devices, on_device(): gram_matrix = lax.psum(local_gram, 'wide')  192 us
    all_gather x2, blocking collectives, back_project(): lax.all_gather(own_share.astype(jnp.bfloat16), 'wide', axis=0, tiled=True)  109 us
    psum x1, waiting for transfers between devices, on_device(): lax.psum(final_part.astype(jnp.bfloat16), 'narrow').astype(jnp.float32)  71.9 us
    psum x1, waiting for transfers between devices, on_device(): feature_image = lax.psum(feature_part.astype(jnp.bfloat16), 'narrow')  71.2 us
    psum x1, waiting for transfers between devices, on_device(): whitened = lax.psum(whitened_part.astype(jnp.bfloat16), 'narrow')  70.5 us
    another operation x6, other arithmetic, on_device(): lower_factor = jnp.linalg.cholesky(gram_matrix)  34 us
  transfers between devices with their start and end apart: 7, of which 7 were waited for; matrix products, arithmetic and copies ran while one was open for 0% of the time, Pallas kernels for 0%

commit v1 on v0

v1 whole, which is shorter than its diff:
```python
import math

import jax
import jax.numpy as jnp
from jax import lax
from jax.experimental import pallas as pl
from jax.experimental.pallas import tpu as pltpu
from jax.sharding import PartitionSpec as P

D = 8192
R = 256
NX, NZ, NY = 4, 8, 8
BF = jnp.bfloat16
F32 = jnp.float32
MESH = pl.DeviceIdType.MESH


def ds(start, size):
    if isinstance(start, int):
        return pl.ds(start, size)
    return pl.ds(pl.multiple_of(start, size), size)


class Rows:
    full, half, xc, zc, dtype = (1024, 256), (512, 256), (128, 256), (16, 256), BF

    @staticmethod
    def x_of(q):
        return (ds(q * 128, 128), slice(None))

    @staticmethod
    def z_of(q):
        return (ds(q * 16, 16), slice(None))

    @staticmethod
    def f_x(c, x):
        return (ds(c * 512 + x * 128, 128), slice(None))

    @staticmethod
    def f_z(c, x, z):
        return (ds(c * 512 + x * 128 + z * 16, 16), slice(None))


class Cols:
    full, half, xc, zc, dtype = (256, 1024), (128, 1024), (32, 1024), (32, 128), BF

    @staticmethod
    def x_of(q):
        return (ds(q * 32, 32), slice(None))

    @staticmethod
    def z_of(q):
        return (slice(None), ds(q * 128, 128))

    @staticmethod
    def f_x(c, x):
        return (ds(c * 128 + x * 32, 32), slice(None))

    @staticmethod
    def f_z(c, x, z):
        return (ds(c * 128 + x * 32, 32), ds(z * 128, 128))


class Gram:
    full, half, xc, zc, dtype = (256, 256), (128, 256), (32, 256), (8, 128), F32

    @staticmethod
    def x_of(q):
        return (ds(q * 32, 32), slice(None))

    @staticmethod
    def z_of(q):
        return (ds((q // 2) * 8, 8), ds((q % 2) * 128, 128))

    @staticmethod
    def f_x(c, x):
        return (ds(c * 128 + x * 32, 32), slice(None))

    @staticmethod
    def f_z(c, x, z):
        return (ds(c * 128 + x * 32 + (z // 2) * 8, 8), ds((z % 2) * 128, 128))


WIDE = (Rows, Cols, Rows, Gram, Cols)
NARROW = (((128, 256), 16), ((256, 832), 32), ((128, 256), 16), ((256, 832), 32))


def wide_scratch(lay):
    vm = pltpu.VMEM
    return [
        vm(lay.half, F32),
        vm(lay.half, lay.dtype),
        vm(lay.half, lay.dtype),
        vm((3,) + lay.xc, lay.dtype),
        vm((3,) + lay.xc, lay.dtype),
        vm(lay.xc, F32),
        vm(lay.xc, lay.dtype),
        vm((7,) + lay.zc, lay.dtype),
        vm(lay.full, lay.dtype),
        pltpu.SemaphoreType.DMA((14,)),
        pltpu.SemaphoreType.DMA((14,)),
    ]


def narrow_scratch(spec):
    shape, rows = spec
    return [
        pltpu.VMEM(shape, BF),
        pltpu.VMEM((rows, shape[1]), F32),
        pltpu.VMEM((7, rows, shape[1]), BF),
        pltpu.VMEM(shape, BF),
        pltpu.SemaphoreType.DMA((2,)),
        pltpu.SemaphoreType.DMA((2,)),
    ]


def dot(a, b):
    return jnp.dot(a, b, preferred_element_type=F32)


def dot_exact(a, b):
    return jnp.dot(a, b, preferred_element_type=F32, precision=lax.Precision.HIGHEST)


class Place:
    def __init__(self):
        w = lax.axis_index("wide")
        self.n = lax.axis_index("narrow")
        self.core = w % 2
        self.x = (w // 2) % NX
        self.z = w // (2 * NX)

    def wide(self, z, x, core):
        return {"wide": (z * NX + x) * 2 + core}

    @property
    def sibling(self):
        return self.wide(self.z, self.x, 1 - self.core)

    def x_peer(self, k):
        return self.wide(self.z, (self.x + k) % NX, self.core)

    def z_peer(self, k):
        return self.wide((self.z + k) % NZ, self.x, self.core)

    def y_peer(self, k):
        return {"narrow": (self.n + k) % NY}


def send(src, dst, ssem, rsem, where):
    copy = pltpu.make_async_remote_copy(
        src_ref=src, dst_ref=dst, send_sem=ssem, recv_sem=rsem, device_id=where, device_id_type=MESH
    )
    copy.start()


def wait_bytes(ref, sem):
    pltpu.make_async_copy(ref, ref, sem).wait()


class WideSum:
    def __init__(self, lay, here, bufs):
        self.lay, self.here = lay, here
        (self.keep, self.csend, self.crecv, self.xsend, self.xrecv, self.own,
         self.zsend, self.zrecv, self.full, self.ss, self.rs) = bufs

    def start(self, make_half, after_first=None):
        lay, here = self.lay, self.here
        self.csend[...] = make_half(1 - here.core).astype(lay.dtype)
        if after_first is not None:
            after_first()
        for k in (2, 1, 3, 0):
            q = lay.x_of((here.x + k) % NX)
            send(self.csend.at[q], self.crecv.at[q], self.ss.at[k], self.rs.at[k], here.sibling)
        self.keep[...] = make_half(here.core)

    def x_step(self):
        lay, here = self.lay, self.here
        for k in (2, 1, 3, 0):
            q = lay.x_of((here.x + k) % NX)
            wait_bytes(self.crecv.at[q], self.rs.at[k])
            total = self.keep[q] + self.crecv[q].astype(F32)
            if k:
                self.xsend[k - 1] = total.astype(lay.dtype)
                send(self.xsend.at[k - 1], self.xrecv.at[k - 1], self.ss.at[4], self.rs.at[4], here.x_peer(k))
            else:
                self.own[...] = total

    def z_step(self):
        lay, here = self.lay, self.here
        wait_bytes(self.xrecv, self.rs.at[4])
        total = self.own[...]
        for k in range(3):
            total = total + self.xrecv[k].astype(F32)
        self.own[...] = total
        self.zsend[...] = total.astype(lay.dtype)
        for k in (4, 3, 5, 2, 6, 1, 7):
            send(self.zsend.at[lay.z_of((here.z + k) % NZ)], self.zrecv.at[k - 1],
                 self.ss.at[5], self.rs.at[5], here.z_peer(k))

    def z_back(self):
        lay, here = self.lay, self.here
        wait_bytes(self.zrecv, self.rs.at[5])
        total = self.own[lay.z_of(here.z)]
        for k in range(7):
            total = total + self.zrecv[k].astype(F32)
        mine = lay.f_z(here.core, here.x, here.z)
        self.full[mine] = total.astype(lay.dtype)
        for k in (4, 3, 5, 2, 6, 1, 7):
            send(self.full.at[mine], self.full.at[mine], self.ss.at[6], self.rs.at[6], here.z_peer(k))

    def x_back(self):
        lay, here = self.lay, self.here
        wait_bytes(self.zrecv, self.rs.at[6])
        mine = lay.f_x(here.core, here.x)
        for k in (2, 1, 3):
            send(self.full.at[mine], self.full.at[mine], self.ss.at[6 + k], self.rs.at[6 + k], here.x_peer(k))
        send(self.full.at[mine], self.full.at[mine], self.ss.at[10], self.rs.at[10], here.sibling)

    def core_back(self):
        lay, here = self.lay, self.here
        for k in (1, 3, 2):
            there = lay.f_x(here.core, (here.x + NX - k) % NX)
            wait_bytes(self.full.at[there], self.rs.at[6 + k])
            send(self.full.at[there], self.full.at[there], self.ss.at[10 + k], self.rs.at[10 + k], here.sibling)

    def finish(self):
        lay, here = self.lay, self.here
        for k in (0, 1, 3, 2):
            there = lay.f_x(1 - here.core, (here.x + NX - k) % NX)
            wait_bytes(self.full.at[there], self.rs.at[10 + k])

    def drain(self):
        lay, here = self.lay, self.here
        for k in range(4):
            wait_bytes(self.csend.at[lay.x_of(k)], self.ss.at[k])
        wait_bytes(self.xsend, self.ss.at[4])
        for j in (5, 6):
            wait_bytes(self.zrecv, self.ss.at[j])
        for j in range(7, 14):
            wait_bytes(self.full.at[lay.f_x(0, 0)], self.ss.at[j])

    def gather(self):
        self.x_step()
        self.z_step()
        self.z_back()
        self.x_back()
        self.core_back()
        self.finish()
        return self.full


class NarrowSum:
    def __init__(self, spec, here, bufs):
        self.rows, self.here = spec[1], here
        self.sendbuf, self.own, self.recv, self.full, self.ss, self.rs = bufs
        self.gathers = False

    def scatter(self, total):
        rows, here = self.rows, self.here
        self.sendbuf[...] = total.astype(BF)
        for k in (4, 3, 5, 2, 6, 1, 7):
            send(self.sendbuf.at[ds(((here.n + k) % NY) * rows, rows)], self.recv.at[k - 1],
                 self.ss.at[0], self.rs.at[0], here.y_peer(k))
        mine = self.sendbuf[ds(here.n * rows, rows)].astype(F32)
        wait_bytes(self.recv, self.rs.at[0])
        for k in range(7):
            mine = mine + self.recv[k].astype(F32)
        return mine

    def gather(self, mine):
        rows, here = self.rows, self.here
        at = ds(here.n * rows, rows)
        self.full[at] = mine.astype(BF)
        for k in (4, 3, 5, 2, 6, 1, 7):
            send(self.full.at[at], self.full.at[at], self.ss.at[1], self.rs.at[1], here.y_peer(k))
        wait_bytes(self.recv, self.rs.at[1])
        self.gathers = True
        return self.full

    def drain(self):
        wait_bytes(self.recv, self.ss.at[0])
        if self.gathers:
            wait_bytes(self.recv, self.ss.at[1])


NB = 32


def inverse_factor(x_ref):
    row = lax.broadcasted_iota(jnp.int32, (NB, 2 * NB), 0)
    col = lax.broadcasted_iota(jnp.int32, (NB, 2 * NB), 1)
    eye = (col == row + NB).astype(F32)
    for b in range(R // NB):
        lo, hi = b * NB, (b + 1) * NB
        block = x_ref[lo:hi, lo:hi]
        e = jnp.concatenate([block, jnp.zeros((NB, NB), F32)], axis=1) + eye
        for j in range(NB - 1):
            pivot = e[j:j + 1, :]
            ratio = e[:, j:j + 1] * (1.0 / e[j:j + 1, j:j + 1])
            e = e - jnp.where(row > j, ratio, 0.0) * pivot
        diag = jnp.sum(jnp.where(row == col, e, 0.0), axis=1, keepdims=True)
        m = e[:, NB:] * lax.rsqrt(diag)
        rows = dot_exact(m, x_ref[lo:hi, :])
        lanes = lax.broadcasted_iota(jnp.int32, (NB, R), 1)
        here = (lanes >= lo) & (lanes < hi)
        wide_m = jnp.concatenate(
            ([jnp.zeros((NB, lo), F32)] if lo else []) + [m] + ([jnp.zeros((NB, R - hi), F32)] if hi < R else []),
            axis=1,
        )
        out = jnp.where(here, wide_m, rows)
        x_ref[lo:hi, :] = out
        if hi < R:
            lower = rows.T[hi:, :]
            rest = x_ref[hi:, :]
            lane = lax.broadcasted_iota(jnp.int32, (R - hi, R), 1)
            rest = jnp.where((lane >= lo) & (lane < hi), 0.0, rest)
            x_ref[hi:, :] = rest - dot_exact(lower, out)


def kernel(w_ref, u_ref, s_ref, basis_ref, proj_ref, *scratch):
    here = Place()
    scratch = list(scratch)
    sums, nsums = [], []
    for lay in WIDE:
        sums.append(WideSum(lay, here, scratch[:11]))
        scratch = scratch[11:]
    for spec in NARROW:
        nsums.append(NarrowSum(spec, here, scratch[:6]))
        scratch = scratch[6:]
    t_ref, y_ref, x_ref = scratch

    barrier = pltpu.get_barrier_semaphore()
    peers = [here.sibling]
    peers += [here.x_peer(k) for k in range(1, NX)]
    peers += [here.z_peer(k) for k in range(1, NZ)]
    peers += [here.y_peer(k) for k in range(1, NY)]
    for peer in peers:
        pl.semaphore_signal(barrier, inc=1, device_id=peer, device_id_type=MESH)

    def enter():
        pl.semaphore_wait(barrier, len(peers))

    def rows_of(ref, size):
        return lambda c: ref[ds(c * size, size), :]

    w_half = rows_of(w_ref, 512)
    t_half = rows_of(t_ref, 128)

    s1 = sums[0]
    s1.start(lambda c: dot(w_half(c), s_ref[...]), enter)
    image = s1.gather()
    n1 = nsums[0]
    mine = n1.scatter(dot(u_ref[...], image[...]))
    whitened = n1.gather(mine)
    t_ref[...] = whitened[...].astype(F32).T.astype(BF)
    s2 = sums[1]
    s2.start(lambda c: dot(t_half(c), u_ref[...]))
    back = s2.gather()
    n2 = nsums[1]
    mine = n2.scatter(dot(back[...], w_ref[...]))
    feature = n2.gather(mine)
    s3 = sums[2]

    def second(c):
        return lax.dot_general(
            w_half(c), feature[...], (((1,), (1,)), ((), ())), preferred_element_type=F32
        )

    s3.start(second)
    image = s3.gather()
    n3 = nsums[2]
    mine = n3.scatter(dot(u_ref[...], image[...]))
    y_ref[...] = mine.astype(BF).astype(F32)
    final = n3.gather(mine)
    t_ref[...] = final[...].astype(F32).T.astype(BF)
    s4, s5 = sums[3], sums[4]
    s4.start(lambda c: dot(t_half(c), final[...]))
    s5.start(lambda c: dot(t_half(c), u_ref[...]))
    for step in ("x_step", "z_step", "z_back", "x_back", "core_back", "finish"):
        getattr(s4, step)()
        getattr(s5, step)()
    x_ref[...] = s4.full[...]
    inverse_factor(x_ref)
    rr = lax.broadcasted_iota(jnp.int32, (R, R), 0)
    cc = lax.broadcasted_iota(jnp.int32, (R, R), 1)
    inverse = jnp.where(cc <= rr, x_ref[...], 0.0)
    x_ref[...] = inverse
    basis_ref[...] = dot_exact(y_ref[...], inverse.T) * math.sqrt(D)
    high = inverse.astype(BF)
    low = (inverse - high.astype(F32)).astype(BF)
    raw = s5.full[...]
    weighted = (dot(high, raw) + dot(low, raw)).astype(BF)
    n4 = nsums[3]
    proj_ref[...] = n4.scatter(dot(weighted, w_ref[...]))
    for s in sums + nsums:
        s.drain()


def on_device(weight, whitening, sketch):
    vmem = pl.BlockSpec(memory_space=pltpu.VMEM)
    scratch = []
    for lay in WIDE:
        scratch += wide_scratch(lay)
    for spec in NARROW:
        scratch += narrow_scratch(spec)
    scratch += [pltpu.VMEM((256, 128), BF), pltpu.VMEM((16, 256), F32), pltpu.VMEM((R, R), F32)]
    return pl.pallas_call(
        kernel,
        out_shape=(
            jax.ShapeDtypeStruct((16, 256), F32),
            jax.ShapeDtypeStruct((32, 832), F32),
        ),
        in_specs=[vmem] * 3,
        out_specs=(vmem, vmem),
        scratch_shapes=scratch,
        compiler_params=pltpu.CompilerParams(
            collective_id=0, has_side_effects=True, vmem_limit_bytes=48 * 1024 * 1024
        ),
        cost_estimate=pl.CostEstimate(flops=2_300_000_000, bytes_accessed=3_000_000, transcendentals=256),
    )(weight, whitening, sketch)


def solution(mesh):
    placed = (P("narrow", "wide"), P("wide", "narrow"), P("wide", None))
    return jax.shard_map(
        on_device,
        mesh=mesh,
        in_specs=placed,
        out_specs=(P(("wide", "narrow"), None), P("narrow", "wide")),
        check_vma=False,
    )
```

time: 1450 us -> 191 us (0.13)
  waiting for transfers between devices: 727 us -> 0 us
  blocking collectives: 626 us -> 0 us
  Pallas kernels: 0 us -> 186 us
  other arithmetic: 57.8 us -> 0 us
  between operations: 15.7 us -> 0.68 us
    psum x2 -> x0, blocking collectives: 517 us -> none  [column_sum(): return lax.psum(partial_image, 'wide').astype(jnp.bfloat16)]
    psum x4 -> x0, waiting for transfers between devices: 406 us -> none  [the longest x1 192 us: on_device(): gram_matrix = lax.psum(local_gram, 'wide')]
    reduce_scatter x3 -> x0, waiting for transfers between devices: 321 us -> none  [the longest x2 290 us: back_project(): lax.psum_scatter(jnp.einsum('ik,ir->kr', whitening, rows_here, preferred_...]
    pallas_call x0 -> x1, Pallas kernels: none -> 186 us  [on_device(): pl.pallas_call(kernel, out_shape=(jax.ShapeDtypeStruct((16, 256), F32), j...]
    all_gather x2 -> x0, blocking collectives: 109 us -> none  [back_project(): lax.all_gather(own_share.astype(jnp.bfloat16), 'wide', axis=0, tiled=True)]
    another operation x9 -> x0, other arithmetic: 53.7 us -> none  [the longest x6 34 us: on_device(): lower_factor = jnp.linalg.cholesky(gram_matrix)]
  transfers between devices with their start and end apart: 7 -> 0, of which waited for: 7 -> 0; matrix products, arithmetic and copies ran while one was open for 0% -> 0% of each run, Pallas kernels for 0% -> 0%
where the time goes in v1:
time: 191 us
  Pallas kernels  186 us (97%)
  local copies, waits for them, and re-layouts  4.36 us (2%)
    pallas_call x1, Pallas kernels, on_device(): pl.pallas_call(kernel, out_shape=(jax.ShapeDtypeStruct((16, 256), F32), j...  186 us
    unnamed x7, local copies, waits for them, and re-layouts  4.36 us

profile of v1, /device:TPU:1, one launch (start us, length us, event | category | flops | bytes accessed | tf_op | source)
XLA Modules:
  0.0 190.6 jit_solution(16372240530896646863)
XLA Ops:
  0.6 0.0 copy-start
  0.6 0.0 copy-start.1
  0.6 3.1 %copy.5.w_ref = bf16[1024,832]{1,0:T(8,128)(2,1)S(1)} copy(bf16[1024,832]{0,1:T(8,128)(2,1)} %param.3) | data formatting | bytes 3407872 | tf_op args[0]
  3.8 0.0 copy-done
  3.8 0.0 copy-done.1
  3.8 185.6 %shard_map.50 = (f32[16,256]{1,0:T(8,128)S(1)}, f32[32,832]{1,0:T(8,128)S(1)}) custom-call(bf16[1024,832]{1,0:T(8,128)(2,1)S(1)} %copy.5.w_ref, bf16[128,1024]{1,0:T(8,128)(2,1)S(1)} %copy-done.1, bf16[832,256]{1,0:T(8,128)(2,1)S(1)} %copy-done), custom_call_target="tpu_custom_call" | custom-call | flops 2300000000 | bytes 3000000 | tf_op jit(solution)/shard_map/pallas_call | solution.py:408
  189.4 0.6 copy.8
  190.0 0.6 copy.9
Async XLA Ops:
  0.6 3.1 %copy-start = (bf16[832,256]{1,0:T(8,128)(2,1)S(1)}, bf16[832,256]{1,0:T(8,128)(2,1)}, u32[]{:S(2)}) copy-start(bf16[832,256]{1,0:T(8,128)(2,1)} %s_ref.1) | copy-start | bytes 1277956
  0.6 3.1 %copy-start.1 = (bf16[128,1024]{1,0:T(8,128)(2,1)S(1)}, bf16[128,1024]{1,0:T(8,128)(2,1)}, u32[]{:S(2)}) copy-start(bf16[128,1024]{1,0:T(8,128)(2,1)} %u_ref.1) | copy-start | bytes 786436

commit v2 on v0

v2 whole, which is shorter than its diff:
```python
import math

import jax
import jax.numpy as jnp
from jax import lax
from jax.experimental import pallas as pl
from jax.experimental.pallas import tpu as pltpu
from jax.sharding import PartitionSpec as P

D = 8192
R = 256
H = 128
NX, NZ, NY = 4, 8, 8
CHAINS = 2
M = H // CHAINS
BF = jnp.bfloat16
F32 = jnp.float32
MESH = pl.DeviceIdType.MESH
FAR_FIRST = (4, 3, 5, 2, 6, 1, 7)
ROUNDS = ("x_step", "z_step", "z_back", "x_back", "finish")


def ds(start, size):
    if isinstance(start, int):
        return pl.ds(start, size)
    return pl.ds(pl.multiple_of(start, size), size)


def dot(a, b):
    return jnp.dot(a, b, preferred_element_type=F32)


def dot_nt(a, b):
    return lax.dot_general(a, b, (((1,), (1,)), ((), ())), preferred_element_type=F32)


def dot_tn(a, b):
    return lax.dot_general(a, b, (((0,), (0,)), ((), ())), preferred_element_type=F32)


def dot_exact(a, b):
    return jnp.dot(a, b, preferred_element_type=F32, precision=lax.Precision.HIGHEST)


class Place:
    def __init__(self):
        w = lax.axis_index("wide")
        self.n = lax.axis_index("narrow")
        self.core = w % 2
        self.x = (w // 2) % NX
        self.z = w // (2 * NX)

    def wide(self, z, x, core):
        return {"wide": (z * NX + x) * 2 + core}

    @property
    def sibling(self):
        return self.wide(self.z, self.x, 1 - self.core)

    def x_peer(self, k):
        return self.wide(self.z, (self.x + k) % NX, self.core)

    def z_peer(self, k):
        return self.wide((self.z + k) % NZ, self.x, self.core)

    def y_peer(self, k):
        return {"narrow": (self.n + k) % NY}


def send(src, dst, ssem, rsem, where):
    copy = pltpu.make_async_remote_copy(
        src_ref=src, dst_ref=dst, send_sem=ssem, recv_sem=rsem, device_id=where, device_id_type=MESH
    )
    copy.start()


def wait_bytes(ref, sem):
    pltpu.make_async_copy(ref, ref, sem).wait()


class Cols:
    dtype = BF

    def __init__(self, base, m):
        self.base, self.m, self.rows = base, m, m // NX
        self.xc, self.zc = (m // NX, 1024), (m // NX, 128)

    def x_of(self, q):
        return (ds(self.base + q * self.rows, self.rows), slice(None))

    def z_of(self, q):
        return (slice(None), ds(q * 128, 128))

    def f_z(self, x, z):
        return (ds(self.base + x * self.rows, self.rows), ds(z * 128, 128))


class Gram:
    dtype, xc, zc = F32, (32, 256), (8, 128)

    def x_of(self, q):
        return (ds(q * 32, 32), slice(None))

    def z_of(self, q):
        return (ds((q // 2) * 8, 8), ds((q % 2) * 128, 128))

    def f_z(self, x, z):
        return (ds(x * 32 + (z // 2) * 8, 8), ds((z % 2) * 128, 128))


def wide_scratch(lay):
    vm = pltpu.VMEM
    return [
        vm((3,) + lay.xc, lay.dtype),
        vm((3,) + lay.xc, lay.dtype),
        vm(lay.xc, F32),
        vm(lay.xc, lay.dtype),
        vm((7,) + lay.zc, lay.dtype),
        pltpu.SemaphoreType.DMA((4,)),
        pltpu.SemaphoreType.DMA((4,)),
    ]


class WideSum:
    def __init__(self, lay, here, bufs, part, full, extra=None):
        self.lay, self.here, self.part, self.full, self.extra = lay, here, part, full, extra
        self.xsend, self.xrecv, self.own, self.zsend, self.zrecv, self.ss, self.rs = bufs
        self.done = 0

    def x_step(self):
        lay, here = self.lay, self.here
        for k in (2, 1, 3, 0):
            q = lay.x_of((here.x + k) % NX)
            total = self.part[q]
            if self.extra is not None:
                total = total + self.extra[q].astype(F32)
            if k:
                self.xsend[k - 1] = total.astype(lay.dtype)
                send(self.xsend.at[k - 1], self.xrecv.at[k - 1], self.ss.at[0], self.rs.at[0], here.x_peer(k))
            else:
                self.own[...] = total
        self.done = 1

    def z_step(self):
        lay, here = self.lay, self.here
        wait_bytes(self.xrecv, self.rs.at[0])
        total = self.own[...]
        for k in range(3):
            total = total + self.xrecv[k].astype(F32)
        self.own[...] = total
        self.zsend[...] = total.astype(lay.dtype)
        for k in FAR_FIRST:
            send(self.zsend.at[lay.z_of((here.z + k) % NZ)], self.zrecv.at[k - 1],
                 self.ss.at[1], self.rs.at[1], here.z_peer(k))
        self.done = 2

    def z_back(self):
        lay, here = self.lay, self.here
        wait_bytes(self.zrecv, self.rs.at[1])
        total = self.own[lay.z_of(here.z)]
        for k in range(7):
            total = total + self.zrecv[k].astype(F32)
        mine = lay.f_z(here.x, here.z)
        self.full[mine] = total.astype(lay.dtype)
        for k in FAR_FIRST:
            send(self.full.at[mine], self.full.at[mine], self.ss.at[2], self.rs.at[2], here.z_peer(k))
        self.done = 3

    def x_back(self):
        lay, here = self.lay, self.here
        wait_bytes(self.zrecv, self.rs.at[2])
        mine = lay.x_of(here.x)
        for k in (2, 1, 3):
            send(self.full.at[mine], self.full.at[mine], self.ss.at[3], self.rs.at[3], here.x_peer(k))
        self.done = 4

    def finish(self):
        wait_bytes(self.xrecv, self.rs.at[3])
        self.done = 5

    def drain(self):
        for i, ref in enumerate((self.xrecv, self.zrecv, self.zrecv, self.xrecv)):
            if self.done > i:
                wait_bytes(ref, self.ss.at[i])
                if self.done == i + 1:
                    wait_bytes(ref, self.rs.at[i])


def narrow_scratch(width):
    return [
        pltpu.VMEM((H, width), BF),
        pltpu.VMEM((7, 16, width), BF),
        pltpu.SemaphoreType.DMA((2,)),
        pltpu.SemaphoreType.DMA((2,)),
    ]


class NarrowSum:
    def __init__(self, here, bufs, full, base=0):
        self.here, self.full, self.base = here, full, base
        self.sendbuf, self.recv, self.ss, self.rs = bufs
        self.done = 0

    def scatter(self, total):
        here = self.here
        self.sendbuf[...] = total.astype(BF)
        for k in FAR_FIRST:
            send(self.sendbuf.at[ds(((here.n + k) % NY) * 16, 16)], self.recv.at[k - 1],
                 self.ss.at[0], self.rs.at[0], here.y_peer(k))
        self.done = 1

    def gather(self):
        here = self.here
        mine = self.sendbuf[ds(here.n * 16, 16)].astype(F32)
        wait_bytes(self.recv, self.rs.at[0])
        for k in range(7):
            mine = mine + self.recv[k].astype(F32)
        at = ds(self.base + here.n * 16, 16)
        self.full[at] = mine.astype(BF)
        for k in FAR_FIRST:
            send(self.full.at[at], self.full.at[at], self.ss.at[1], self.rs.at[1], here.y_peer(k))
        self.done = 2

    def finish(self):
        wait_bytes(self.recv, self.rs.at[1])
        self.done = 3

    def drain(self):
        for i in range(2):
            if self.done > i:
                wait_bytes(self.recv, self.ss.at[i])
                if self.done == i + 1:
                    wait_bytes(self.recv, self.rs.at[i])


NB = 32


def inverse_factor(x_ref):
    row = lax.broadcasted_iota(jnp.int32, (NB, 2 * NB), 0)
    col = lax.broadcasted_iota(jnp.int32, (NB, 2 * NB), 1)
    eye = (col == row + NB).astype(F32)
    for b in range(R // NB):
        lo, hi = b * NB, (b + 1) * NB
        block = x_ref[lo:hi, lo:hi]
        e = jnp.concatenate([block, jnp.zeros((NB, NB), F32)], axis=1) + eye
        for j in range(NB - 1):
            pivot = e[j:j + 1, :]
            ratio = e[:, j:j + 1] * (1.0 / e[j:j + 1, j:j + 1])
            e = e - jnp.where(row > j, ratio, 0.0) * pivot
        diag = jnp.sum(jnp.where(row == col, e, 0.0), axis=1, keepdims=True)
        m = e[:, NB:] * lax.rsqrt(diag)
        rows = dot_exact(m, x_ref[lo:hi, :])
        lanes = lax.broadcasted_iota(jnp.int32, (NB, R), 1)
        wide_m = jnp.concatenate(
            ([jnp.zeros((NB, lo), F32)] if lo else []) + [m] + ([jnp.zeros((NB, R - hi), F32)] if hi < R else []),
            axis=1,
        )
        out = jnp.where((lanes >= lo) & (lanes < hi), wide_m, rows)
        x_ref[lo:hi, :] = out
        if hi < R:
            lower = rows.T[hi:, :]
            rest = x_ref[hi:, :]
            lane = lax.broadcasted_iota(jnp.int32, (R - hi, R), 1)
            rest = jnp.where((lane >= lo) & (lane < hi), 0.0, rest)
            x_ref[hi:, :] = rest - dot_exact(lower, out)
        yield b


CHAIN = [Cols(g * M, M) for g in range(CHAINS)]
ONE = Cols(0, H)
WIDE = CHAIN + CHAIN + CHAIN + [ONE, Gram()]
NARROW = (256, 832, 832, 256)


def body(wt_hbm, u_hbm, s_hbm, basis_ref, proj_ref, scratch, drains):
    here = Place()
    core, n = here.core, here.n
    scratch = list(scratch)

    def take(count):
        got = scratch[:count]
        del scratch[:count]
        return got

    wide_bufs = [take(7) for _ in WIDE]
    narrow_bufs = [take(4) for _ in NARROW]
    (wt2, u2, s_ref, csend, crecv, part, img1, img2, img3, img4, gpart, gfull, v_ref, c2, ya, yb, x_ref,
     zbuf, zrecv, zpair, zall, pbuf, precv) = take(23)
    lsem, psem, qsem = take(3)

    barrier = pltpu.get_barrier_semaphore()
    peers = [here.sibling]
    peers += [here.x_peer(k) for k in range(1, NX)]
    peers += [here.z_peer(k) for k in range(1, NZ)]
    peers += [here.y_peer(k) for k in range(1, NY)]
    for peer in peers:
        pl.semaphore_signal(barrier, inc=1, device_id=peer, device_id_type=MESH)
    loads = [
        pltpu.make_async_copy(wt_hbm, wt2.at[core], lsem.at[0]),
        pltpu.make_async_copy(s_hbm, s_ref, lsem.at[1]),
        pltpu.make_async_copy(u_hbm, u2.at[ds(core * H, H)], lsem.at[2]),
    ]
    for load in loads:
        load.start()
    zbuf[...] = jnp.zeros_like(zbuf)
    for load in loads:
        load.wait()

    def first(c):
        return dot_tn(s_ref[:, ds(c * H, H)], wt2[core])

    csend[...] = first(1 - core).astype(BF)
    pl.semaphore_wait(barrier, len(peers))
    send(csend, crecv, psem.at[0], qsem.at[0], here.sibling)
    mine_u = u2.at[ds(core * H, H)]
    send(wt2.at[core], wt2.at[core], psem.at[1], qsem.at[1], here.sibling)
    send(mine_u, mine_u, psem.at[2], qsem.at[2], here.sibling)
    drains.append(lambda: wait_bytes(csend, psem.at[0]))
    drains.append(lambda: wait_bytes(wt2.at[0], psem.at[1]))
    drains.append(lambda: wait_bytes(u2.at[0:H], psem.at[2]))
    part[...] = first(core)
    wait_bytes(crecv, qsem.at[0])
    yield "start"

    sums = []

    def wide(index, full, parts=part, extra=None):
        got = WideSum(WIDE[index], here, wide_bufs[index], parts, full, extra)
        drains.append(got.drain)
        return got

    def run(chain):
        for step in ROUNDS:
            for s in chain:
                getattr(s, step)()
            yield step

    def narrow(index, full, base=0):
        got = NarrowSum(here, narrow_bufs[index], full, base)
        drains.append(got.drain)
        return got

    yield from run([wide(g, img1, extra=crecv) for g in range(CHAINS)])
    wait_bytes(u2.at[0:H], qsem.at[2])
    n1 = narrow(0, v_ref)
    n1.scatter(dot_nt(img1[...], u2[...]))
    yield "n1s"
    n1.gather()
    yield "n1g"
    n1.finish()
    part[...] = dot(v_ref[...], u2[...])
    yield from run([wide(CHAINS + g, img2) for g in range(CHAINS)])
    wait_bytes(wt2.at[0], qsem.at[1])
    n2 = [narrow(1 + b, c2.at[b]) for b in range(2)]
    for b in range(2):
        n2[b].scatter(dot_nt(img2[...], wt2[b]))
    yield "n2s"
    for b in range(2):
        n2[b].gather()
    yield "n2g"
    n2[0].finish()
    part[...] = dot(c2[0], wt2[0])
    n2[1].finish()
    part[...] += dot(c2[1], wt2[1])
    yield from run([wide(2 * CHAINS + g, img3) for g in range(CHAINS)])
    n3 = narrow(3, ya, core * H)
    n3.scatter(dot_nt(img3[...], u2[...]))
    yield "n3s"
    n3.gather()
    yield "n3g"
    n3.finish()
    mine_y = ya.at[ds(core * H, H)]
    send(mine_y, mine_y, psem.at[3], qsem.at[3], here.sibling)
    drains.append(lambda: wait_bytes(ya.at[0:H], psem.at[3]))
    part[...] = dot(mine_y[...], u2[...])
    wait_bytes(ya.at[0:H], qsem.at[3])
    gpart[...] = dot_nt(mine_y[...], ya[...])
    gfull_mine = gfull.at[ds(core * H, H)]
    gram = wide(3 * CHAINS + 1, gfull_mine, gpart)
    last = wide(3 * CHAINS, img4)
    yield "y"
    gram.x_step()
    last.x_step()
    yb[...] = ya[...].astype(F32).T
    yield "gx"
    gram.z_step()
    last.z_step()
    yield "gz"
    gram.z_back()
    last.z_back()
    yield "gzb"
    gram.x_back()
    last.x_back()
    yield "gxb"
    gram.finish()
    send(gfull_mine, gfull_mine, psem.at[4], qsem.at[4], here.sibling)
    drains.append(lambda: wait_bytes(gfull.at[0:H], psem.at[4]))
    wait_bytes(gfull.at[0:H], qsem.at[4])
    yield "gram"
    x_ref[...] = gfull[...]
    factor = inverse_factor(x_ref)
    next(factor)
    last.finish()
    for b in range(2):
        zbuf[b, :, 0:832] = dot_nt(img4[...], wt2[b]).astype(BF)
    for k in FAR_FIRST:
        to = (n + k) % NY

        @pl.when(to < 7)
        def _():
            send(zbuf.at[:, :, ds(to * 128, 128)], zrecv.at[k - 1], psem.at[5], qsem.at[5], here.y_peer(k))

    def drain_z():
        @pl.when(n < 7)
        def _():
            wait_bytes(zrecv.at[0:6], psem.at[5])

        @pl.when(n == 7)
        def _():
            wait_bytes(zrecv, psem.at[5])

    drains.append(drain_z)
    for _ in range(5):
        next(factor)

    @pl.when(n < 7)
    def _():
        wait_bytes(zrecv, qsem.at[5])
        total = zbuf[:, :, ds(n * 128, 128)].astype(F32)
        for k in range(7):
            total = total + zrecv[k].astype(F32)
        zpair[...] = total.astype(BF)
        to = zall.at[ds(core * H, H)]
        send(zpair.at[1 - core], to, psem.at[6], qsem.at[6], here.sibling)
        to[...] = zpair[core]

    for _ in factor:
        pass
    rr = lax.broadcasted_iota(jnp.int32, (R, R), 0)
    cc = lax.broadcasted_iota(jnp.int32, (R, R), 1)
    inverse = jnp.where(cc <= rr, x_ref[...], 0.0)
    yield "factor"
    high = inverse.astype(BF)
    low = (inverse - high.astype(F32)).astype(BF)

    @pl.when(n < 7)
    def _():
        wait_bytes(zpair.at[0], qsem.at[6])
        pbuf[...] = (dot(high, zall[...]) + dot(low, zall[...])).astype(BF)
        for k in FAR_FIRST:
            send(pbuf.at[ds(((n + k) % NY) * 32, 32)], precv.at[n], psem.at[7], qsem.at[7], here.y_peer(k))
        precv[n] = pbuf[ds(n * 32, 32)]

    rows = yb[ds(core * H + n * 16, 16), :]
    basis_ref[...] = lax.dot_general(
        rows, inverse, (((1,), (1,)), ((), ())), preferred_element_type=F32, precision=lax.Precision.HIGHEST
    ) * math.sqrt(D)

    @pl.when(n < 7)
    def _():
        wait_bytes(precv.at[0:6], qsem.at[7])

    @pl.when(n == 7)
    def _():
        wait_bytes(precv, qsem.at[7])

    for j in range(6):
        proj_ref[:, j * 128:(j + 1) * 128] = precv[j].astype(F32)
    proj_ref[:, 768:832] = precv[6][:, 0:64].astype(F32)

    @pl.when(n < 7)
    def _():
        wait_bytes(zpair.at[0], psem.at[6])
        wait_bytes(precv, psem.at[7])

    yield "end"


def kernel(wt_hbm, u_hbm, s_hbm, basis_ref, proj_ref, *scratch):
    drains = []
    for _ in body(wt_hbm, u_hbm, s_hbm, basis_ref, proj_ref, scratch, drains):
        pass
    for drain in drains:
        drain()


def on_device(weight, whitening, sketch):
    vmem = pl.BlockSpec(memory_space=pltpu.VMEM)
    hbm = pl.BlockSpec(memory_space=pl.ANY)
    vm = pltpu.VMEM
    scratch = []
    for lay in WIDE:
        scratch += wide_scratch(lay)
    for width in NARROW:
        scratch += narrow_scratch(width)
    scratch += [
        vm((2, 832, 1024), BF),
        vm((2 * H, 1024), BF),
        vm((832, R), BF),
        vm((H, 1024), BF),
        vm((H, 1024), BF),
        vm((H, 1024), F32),
        vm((H, 1024), BF),
        vm((H, 1024), BF),
        vm((H, 1024), BF),
        vm((H, 1024), BF),
        vm((H, R), F32),
        vm((R, R), F32),
        vm((H, 2 * H), BF),
        vm((2, H, 832), BF),
        vm((R, 2 * H), BF),
        vm((2 * H, R), F32),
        vm((R, R), F32),
        vm((2, H, 896), BF),
        vm((7, 2, H, 128), BF),
        vm((2, H, 128), BF),
        vm((R, 128), BF),
        vm((R, 128), BF),
        vm((7, 32, 128), BF),
        pltpu.SemaphoreType.DMA((3,)),
        pltpu.SemaphoreType.DMA((8,)),
        pltpu.SemaphoreType.DMA((8,)),
    ]
    return pl.pallas_call(
        kernel,
        out_shape=(
            jax.ShapeDtypeStruct((16, R), F32),
            jax.ShapeDtypeStruct((32, 832), F32),
        ),
        in_specs=[hbm] * 3,
        out_specs=(vmem, vmem),
        scratch_shapes=scratch,
        compiler_params=pltpu.CompilerParams(
            collective_id=0, has_side_effects=True, vmem_limit_bytes=48 * 1024 * 1024
        ),
        cost_estimate=pl.CostEstimate(flops=2_300_000_000, bytes_accessed=3_000_000, transcendentals=256),
    )(weight.T, whitening, sketch)


def solution(mesh):
    placed = (P("narrow", "wide"), P("wide", "narrow"), P("wide", None))
    return jax.shard_map(
        on_device,
        mesh=mesh,
        in_specs=placed,
        out_specs=(P(("wide", "narrow"), None), P("narrow", "wide")),
        check_vma=False,
    )
```

time: 1450 us -> 165 us (0.11)
  waiting for transfers between devices: 727 us -> 0 us
  blocking collectives: 626 us -> 0 us
  Pallas kernels: 0 us -> 159 us
  other arithmetic: 57.8 us -> 0 us
  between operations: 15.7 us -> 0.65 us
    psum x2 -> x0, blocking collectives: 517 us -> none  [column_sum(): return lax.psum(partial_image, 'wide').astype(jnp.bfloat16)]
    psum x4 -> x0, waiting for transfers between devices: 406 us -> none  [the longest x1 192 us: on_device(): gram_matrix = lax.psum(local_gram, 'wide')]
    reduce_scatter x3 -> x0, waiting for transfers between devices: 321 us -> none  [the longest x2 290 us: back_project(): lax.psum_scatter(jnp.einsum('ik,ir->kr', whitening, rows_here, preferred_...]
    pallas_call x0 -> x1, Pallas kernels: none -> 159 us  [on_device(): pl.pallas_call(kernel, out_shape=(jax.ShapeDtypeStruct((16, R), F32), jax...]
    all_gather x2 -> x0, blocking collectives: 109 us -> none  [back_project(): lax.all_gather(own_share.astype(jnp.bfloat16), 'wide', axis=0, tiled=True)]
    another operation x9 -> x0, other arithmetic: 53.7 us -> none  [the longest x6 34 us: on_device(): lower_factor = jnp.linalg.cholesky(gram_matrix)]
  transfers between devices with their start and end apart: 7 -> 0, of which waited for: 7 -> 0; matrix products, arithmetic and copies ran while one was open for 0% -> 0% of each run, Pallas kernels for 0% -> 0%
where the time goes in v2:
time: 165 us
  Pallas kernels  159 us (96%)
  local copies, waits for them, and re-layouts  4.66 us (3%)
    pallas_call x1, Pallas kernels, on_device(): pl.pallas_call(kernel, out_shape=(jax.ShapeDtypeStruct((16, R), F32), jax...  159 us
    unnamed x8, local copies, waits for them, and re-layouts  4.66 us

profile of v2, /device:TPU:1, one launch (start us, length us, event | category | flops | bytes accessed | tf_op | source)
XLA Modules:
  0.0 164.7 jit_solution(16420547684327893165)
XLA Ops:
  0.6 0.0 copy-start
  0.6 1.4 copy-done
  2.1 0.0 copy-start.1
  2.1 1.0 copy-done.1
  3.1 0.0 copy-start.2
  3.1 0.9 copy-done.2
  4.0 159.4 %shard_map.50 = (f32[16,256]{1,0:T(8,128)S(1)}, f32[32,832]{1,0:T(8,128)S(1)}) custom-call(bf16[832,1024]{1,0:T(8,128)(2,1)S(1)} %bitcast.1, bf16[128,1024]{1,0:T(8,128)(2,1)S(1)} %copy-done.2, bf16[832,256]{1,0:T(8,128)(2,1)S(1)} %copy-done.1), custom_call_target="tpu_custom_call" | custom-call | flops 2300000000 | bytes 3000000 | tf_op jit(solution)/shard_map/pallas_call | solution.py:525
  163.4 0.6 copy.7
  164.1 0.6 copy.8
Async XLA Ops:
  0.6 1.5 copy-start
  2.1 1.0 copy-start.1
  3.1 0.9 copy-start.2

commit v3 on v2

--- a/solution.py
+++ b/solution.py
@@ -36,10 +36,6 @@
 
 def dot_tn(a, b):
     return lax.dot_general(a, b, (((0,), (0,)), ((), ())), preferred_element_type=F32)
-
-
-def dot_exact(a, b):
-    return jnp.dot(a, b, preferred_element_type=F32, precision=lax.Precision.HIGHEST)
 
 
 class Place:
@@ -234,36 +230,58 @@
 
 
 NB = 32
+GROUP = 8
+
+
+def thirds(a):
+    first = a.astype(BF)
+    rest = a - first.astype(F32)
+    second = rest.astype(BF)
+    return first, second, (rest - second.astype(F32)).astype(BF)
+
+
+def dot_thirds(a, b):
+    a1, a2, a3 = thirds(a)
+    b1, b2, b3 = thirds(b)
+    return dot(
+        jnp.concatenate([a1, a1, a2, a2, a1, a3], axis=1),
+        jnp.concatenate([b1, b2, b1, b2, b3, b1], axis=0),
+    )
+
+
+def block_inverse(block):
+    shape = (NB, 2 * NB)
+    row = lax.broadcasted_iota(jnp.int32, shape, 0)
+    col = lax.broadcasted_iota(jnp.int32, shape, 1)
+    e = jnp.concatenate([block, jnp.zeros((NB, NB), F32)], axis=1) + (col == row + NB).astype(F32)
+    for start in range(0, NB, GROUP):
+        spread = [jnp.broadcast_to(e[:, start + j:start + j + 1], shape) for j in range(GROUP)]
+        for p in range(GROUP):
+            at = slice(start + p, start + p + 1)
+            ratio = jnp.where(row > start + p, spread[p] * (1.0 / spread[p][at]), 0.0)
+            for m in range(p + 1, GROUP):
+                spread[m] = spread[m] - ratio * spread[m][at]
+            e = e - ratio * e[at]
+    diagonal = jnp.sum(jnp.where(row == col, e, 0.0), axis=1, keepdims=True)
+    return e[:, NB:] * lax.rsqrt(diagonal)
 
 
 def inverse_factor(x_ref):
-    row = lax.broadcasted_iota(jnp.int32, (NB, 2 * NB), 0)
-    col = lax.broadcasted_iota(jnp.int32, (NB, 2 * NB), 1)
-    eye = (col == row + NB).astype(F32)
     for b in range(R // NB):
         lo, hi = b * NB, (b + 1) * NB
-        block = x_ref[lo:hi, lo:hi]
-        e = jnp.concatenate([block, jnp.zeros((NB, NB), F32)], axis=1) + eye
-        for j in range(NB - 1):
-            pivot = e[j:j + 1, :]
-            ratio = e[:, j:j + 1] * (1.0 / e[j:j + 1, j:j + 1])
-            e = e - jnp.where(row > j, ratio, 0.0) * pivot
-        diag = jnp.sum(jnp.where(row == col, e, 0.0), axis=1, keepdims=True)
-        m = e[:, NB:] * lax.rsqrt(diag)
-        rows = dot_exact(m, x_ref[lo:hi, :])
-        lanes = lax.broadcasted_iota(jnp.int32, (NB, R), 1)
-        wide_m = jnp.concatenate(
-            ([jnp.zeros((NB, lo), F32)] if lo else []) + [m] + ([jnp.zeros((NB, R - hi), F32)] if hi < R else []),
-            axis=1,
-        )
-        out = jnp.where((lanes >= lo) & (lanes < hi), wide_m, rows)
+        m = block_inverse(x_ref[lo:hi, lo:hi])
+        rows = dot_thirds(m, x_ref[lo:hi, :])
+        lane = lax.broadcasted_iota(jnp.int32, (NB, R), 1)
+        pieces = [jnp.zeros((NB, lo), F32)] if lo else []
+        pieces.append(m)
+        if hi < R:
+            pieces.append(jnp.zeros((NB, R - hi), F32))
+        out = jnp.where((lane >= lo) & (lane < hi), jnp.concatenate(pieces, axis=1), rows)
         x_ref[lo:hi, :] = out
         if hi < R:
-            lower = rows.T[hi:, :]
-            rest = x_ref[hi:, :]
             lane = lax.broadcasted_iota(jnp.int32, (R - hi, R), 1)
-            rest = jnp.where((lane >= lo) & (lane < hi), 0.0, rest)
-            x_ref[hi:, :] = rest - dot_exact(lower, out)
+            rest = jnp.where((lane >= lo) & (lane < hi), 0.0, x_ref[hi:, :])
+            x_ref[hi:, :] = rest - dot_thirds(rows.T[hi:, :], out)
         yield b
 
 
@@ -398,41 +416,43 @@
     drains.append(lambda: wait_bytes(gfull.at[0:H], psem.at[4]))
     wait_bytes(gfull.at[0:H], qsem.at[4])
     yield "gram"
-    x_ref[...] = gfull[...]
-    factor = inverse_factor(x_ref)
-    next(factor)
     last.finish()
     for b in range(2):
         zbuf[b, :, 0:832] = dot_nt(img4[...], wt2[b]).astype(BF)
-    for k in FAR_FIRST:
-        to = (n + k) % NY
-
-        @pl.when(to < 7)
-        def _():
-            send(zbuf.at[:, :, ds(to * 128, 128)], zrecv.at[k - 1], psem.at[5], qsem.at[5], here.y_peer(k))
+        for k in FAR_FIRST:
+            to = (n + k) % NY
+
+            @pl.when(to < 7)
+            def _():
+                send(zbuf.at[b, :, ds(to * 128, 128)], zrecv.at[b, k - 1], psem.at[5 + b], qsem.at[5 + b], here.y_peer(k))
 
     def drain_z():
-        @pl.when(n < 7)
-        def _():
-            wait_bytes(zrecv.at[0:6], psem.at[5])
-
-        @pl.when(n == 7)
-        def _():
-            wait_bytes(zrecv, psem.at[5])
+        for b in range(2):
+
+            @pl.when(n < 7)
+            def _():
+                wait_bytes(zrecv.at[b, 0:6], psem.at[5 + b])
+
+            @pl.when(n == 7)
+            def _():
+                wait_bytes(zrecv.at[b], psem.at[5 + b])
 
     drains.append(drain_z)
+    x_ref[...] = gfull[...]
+    factor = inverse_factor(x_ref)
     for _ in range(5):
         next(factor)
 
     @pl.when(n < 7)
     def _():
-        wait_bytes(zrecv, qsem.at[5])
-        total = zbuf[:, :, ds(n * 128, 128)].astype(F32)
-        for k in range(7):
-            total = total + zrecv[k].astype(F32)
-        zpair[...] = total.astype(BF)
+        for b in range(2):
+            wait_bytes(zrecv.at[b], qsem.at[5 + b])
+            total = zbuf[b, :, ds(n * 128, 128)].astype(F32)
+            for k in range(7):
+                total = total + zrecv[b, k].astype(F32)
+            zpair[b] = total.astype(BF)
         to = zall.at[ds(core * H, H)]
-        send(zpair.at[1 - core], to, psem.at[6], qsem.at[6], here.sibling)
+        send(zpair.at[1 - core], to, psem.at[8], qsem.at[8], here.sibling)
         to[...] = zpair[core]
 
     for _ in factor:
@@ -446,7 +466,7 @@
 
     @pl.when(n < 7)
     def _():
-        wait_bytes(zpair.at[0], qsem.at[6])
+        wait_bytes(zpair.at[0], qsem.at[8])
         pbuf[...] = (dot(high, zall[...]) + dot(low, zall[...])).astype(BF)
         for k in FAR_FIRST:
             send(pbuf.at[ds(((n + k) % NY) * 32, 32)], precv.at[n], psem.at[7], qsem.at[7], here.y_peer(k))
@@ -471,7 +491,7 @@
 
     @pl.when(n < 7)
     def _():
-        wait_bytes(zpair.at[0], psem.at[6])
+        wait_bytes(zpair.at[0], psem.at[8])
         wait_bytes(precv, psem.at[7])
 
     yield "end"
@@ -513,14 +533,14 @@
         vm((2 * H, R), F32),
         vm((R, R), F32),
         vm((2, H, 896), BF),
-        vm((7, 2, H, 128), BF),
+        vm((2, 7, H, 128), BF),
         vm((2, H, 128), BF),
         vm((R, 128), BF),
         vm((R, 128), BF),
         vm((7, 32, 128), BF),
         pltpu.SemaphoreType.DMA((3,)),
-        pltpu.SemaphoreType.DMA((8,)),
-        pltpu.SemaphoreType.DMA((8,)),
+        pltpu.SemaphoreType.DMA((9,)),
+        pltpu.SemaphoreType.DMA((9,)),
     ]
     return pl.pallas_call(
         kernel,

time: 165 us -> 156 us (0.945); the launches traced: 165 us -> 153 us
  Pallas kernels: 159 us -> 148 us
    pallas_call x1, Pallas kernels: 159 us -> 148 us  [on_device(): pl.pallas_call(kernel, out_shape=(jax.ShapeDtypeStruct((16, R), F32), jax...]
where the time goes in v3:
time: 156 us; the launch traced here: 153 us
  Pallas kernels  148 us (95%)
  local copies, waits for them, and re-layouts  4.66 us (3%)
    pallas_call x1, Pallas kernels, on_device(): pl.pallas_call(kernel, out_shape=(jax.ShapeDtypeStruct((16, R), F32), jax...  148 us
    unnamed x8, local copies, waits for them, and re-layouts  4.66 us

profile of v3, /device:TPU:1, one launch (start us, length us, event | category | flops | bytes accessed | tf_op | source)
XLA Modules:
  0.0 153.1 jit_solution(15628103610161400157)
XLA Ops:
  0.6 0.0 copy-start
  0.6 1.4 copy-done
  2.1 0.0 copy-start.1
  2.1 1.0 copy-done.1
  3.1 0.0 copy-start.2
  3.1 0.9 copy-done.2
  4.0 147.8 %shard_map.50 = (f32[16,256]{1,0:T(8,128)S(1)}, f32[32,832]{1,0:T(8,128)S(1)}) custom-call(bf16[832,1024]{1,0:T(8,128)(2,1)S(1)} %bitcast.1, bf16[128,1024]{1,0:T(8,128)(2,1)S(1)} %copy-done.2, bf16[832,256]{1,0:T(8,128)(2,1)S(1)} %copy-done.1), custom_call_target="tpu_custom_call" | custom-call | flops 2300000000 | bytes 3000000 | tf_op jit(solution)/shard_map/pallas_call | solution.py:545
  151.9 0.6 copy.7
  152.5 0.6 copy.8
Async XLA Ops:
  0.6 1.5 copy-start
  2.1 1.0 copy-start.1
  3.1 0.9 copy-start.2

commit v4 on v3

--- a/solution.py
+++ b/solution.py
@@ -89,19 +89,6 @@
 
     def f_z(self, x, z):
         return (ds(self.base + x * self.rows, self.rows), ds(z * 128, 128))
-
-
-class Gram:
-    dtype, xc, zc = F32, (32, 256), (8, 128)
-
-    def x_of(self, q):
-        return (ds(q * 32, 32), slice(None))
-
-    def z_of(self, q):
-        return (ds((q // 2) * 8, 8), ds((q % 2) * 128, 128))
-
-    def f_z(self, x, z):
-        return (ds(x * 32 + (z // 2) * 8, 8), ds((z % 2) * 128, 128))
 
 
 def wide_scratch(lay):
@@ -182,6 +169,78 @@
                     wait_bytes(ref, self.rs.at[i])
 
 
+GROWS = 3 * H // 2
+GZ = GROWS // NZ
+
+
+def gram_scratch():
+    vm = pltpu.VMEM
+    return [
+        vm((GROWS, H), F32),
+        vm((7, GZ, H), F32),
+        vm((NX, GZ, H), F32),
+        vm((2, GROWS, H), F32),
+        pltpu.SemaphoreType.DMA((4,)),
+        pltpu.SemaphoreType.DMA((4,)),
+    ]
+
+
+class GramSum:
+    def __init__(self, here, bufs):
+        self.here = here
+        self.part, self.zrecv, self.xall, self.full, self.ss, self.rs = bufs
+        self.done = 0
+
+    def z_step(self):
+        here = self.here
+        for k in FAR_FIRST:
+            send(self.part.at[ds(((here.z + k) % NZ) * GZ, GZ)], self.zrecv.at[k - 1],
+                 self.ss.at[0], self.rs.at[0], here.z_peer(k))
+        self.done = 1
+
+    def x_step(self):
+        here = self.here
+        wait_bytes(self.zrecv, self.rs.at[0])
+        total = self.part[ds(here.z * GZ, GZ)]
+        for k in range(7):
+            total = total + self.zrecv[k]
+        mine = self.xall.at[here.x]
+        mine[...] = total
+        for k in (2, 1, 3):
+            send(mine, mine, self.ss.at[1], self.rs.at[1], here.x_peer(k))
+        self.done = 2
+
+    def z_back(self):
+        here = self.here
+        wait_bytes(self.xall.at[0:3], self.rs.at[1])
+        total = self.xall[0]
+        for k in range(1, NX):
+            total = total + self.xall[k]
+        mine = self.full.at[here.core, ds(here.z * GZ, GZ)]
+        mine[...] = total
+        for k in FAR_FIRST:
+            send(mine, mine, self.ss.at[2], self.rs.at[2], here.z_peer(k))
+        self.done = 3
+
+    def core_back(self):
+        here = self.here
+        wait_bytes(self.zrecv, self.rs.at[2])
+        mine = self.full.at[here.core]
+        send(mine, mine, self.ss.at[3], self.rs.at[3], here.sibling)
+        self.done = 4
+
+    def finish(self):
+        wait_bytes(self.part, self.rs.at[3])
+        self.done = 5
+
+    def drain(self):
+        for i, ref in enumerate((self.zrecv, self.xall.at[0:3], self.zrecv, self.part)):
+            if self.done > i:
+                wait_bytes(ref, self.ss.at[i])
+                if self.done == i + 1:
+                    wait_bytes(ref, self.rs.at[i])
+
+
 def narrow_scratch(width):
     return [
         pltpu.VMEM((H, width), BF),
@@ -229,8 +288,8 @@
                     wait_bytes(self.recv, self.rs.at[i])
 
 
-NB = 32
-GROUP = 8
+NB = 64
+GROUP = 16
 
 
 def thirds(a):
@@ -254,14 +313,19 @@
     row = lax.broadcasted_iota(jnp.int32, shape, 0)
     col = lax.broadcasted_iota(jnp.int32, shape, 1)
     e = jnp.concatenate([block, jnp.zeros((NB, NB), F32)], axis=1) + (col == row + NB).astype(F32)
+    done = []
     for start in range(0, NB, GROUP):
-        spread = [jnp.broadcast_to(e[:, start + j:start + j + 1], shape) for j in range(GROUP)]
+        left = row[:NB - start]
+        spread = [jnp.broadcast_to(e[:, start + j:start + j + 1], e.shape) for j in range(GROUP)]
         for p in range(GROUP):
-            at = slice(start + p, start + p + 1)
-            ratio = jnp.where(row > start + p, spread[p] * (1.0 / spread[p][at]), 0.0)
+            at = slice(p, p + 1)
+            ratio = jnp.where(left > p, spread[p] * (1.0 / spread[p][at]), 0.0)
             for m in range(p + 1, GROUP):
                 spread[m] = spread[m] - ratio * spread[m][at]
             e = e - ratio * e[at]
+        done.append(e[:GROUP])
+        e = e[GROUP:]
+    e = jnp.concatenate(done, axis=0)
     diagonal = jnp.sum(jnp.where(row == col, e, 0.0), axis=1, keepdims=True)
     return e[:, NB:] * lax.rsqrt(diagonal)
 
@@ -286,8 +350,7 @@
 
 
 CHAIN = [Cols(g * M, M) for g in range(CHAINS)]
-ONE = Cols(0, H)
-WIDE = CHAIN + CHAIN + CHAIN + [ONE, Gram()]
+WIDE = CHAIN * 4
 NARROW = (256, 832, 832, 256)
 
 
@@ -303,9 +366,10 @@
 
     wide_bufs = [take(7) for _ in WIDE]
     narrow_bufs = [take(4) for _ in NARROW]
-    (wt2, u2, s_ref, csend, crecv, part, img1, img2, img3, img4, gpart, gfull, v_ref, c2, ya, yb, x_ref,
-     zbuf, zrecv, zpair, zall, pbuf, precv) = take(23)
-    lsem, psem, qsem = take(3)
+    gram_bufs = take(6)
+    (wt2, u2, s_ref, csend, crecv, part, img1, img2, img3, img4, v_ref, c2, ya, yb, x_ref,
+     zbuf, zrecv, zpair, zall, pbuf, precv) = take(21)
+    lsem, zss, zrs, psem, qsem = take(5)
 
     barrier = pltpu.get_barrier_semaphore()
     peers = [here.sibling]
@@ -392,65 +456,75 @@
     send(mine_y, mine_y, psem.at[3], qsem.at[3], here.sibling)
     drains.append(lambda: wait_bytes(ya.at[0:H], psem.at[3]))
     part[...] = dot(mine_y[...], u2[...])
+    last = [wide(3 * CHAINS + g, img4) for g in range(CHAINS)]
+    for t in last:
+        t.x_step()
+    gram = GramSum(here, gram_bufs)
+    drains.append(gram.drain)
     wait_bytes(ya.at[0:H], qsem.at[3])
-    gpart[...] = dot_nt(mine_y[...], ya[...])
-    gfull_mine = gfull.at[ds(core * H, H)]
-    gram = wide(3 * CHAINS + 1, gfull_mine, gpart)
-    last = wide(3 * CHAINS, img4)
-    yield "y"
-    gram.x_step()
-    last.x_step()
+    gram.part[0:H] = dot_nt(mine_y[...], mine_y[...])
+    gram.part[H:GROWS] = dot_nt(ya[ds(core * (H // 2), H // 2)], ya[H:R])
+    gram.z_step()
     yb[...] = ya[...].astype(F32).T
     yield "gx"
-    gram.z_step()
-    last.z_step()
+    for t in last:
+        t.z_step()
+    gram.x_step()
     yield "gz"
+    for t in last:
+        t.z_back()
     gram.z_back()
-    last.z_back()
     yield "gzb"
-    gram.x_back()
-    last.x_back()
-    yield "gxb"
-    gram.finish()
-    send(gfull_mine, gfull_mine, psem.at[4], qsem.at[4], here.sibling)
-    drains.append(lambda: wait_bytes(gfull.at[0:H], psem.at[4]))
-    wait_bytes(gfull.at[0:H], qsem.at[4])
-    yield "gram"
-    last.finish()
-    for b in range(2):
-        zbuf[b, :, 0:832] = dot_nt(img4[...], wt2[b]).astype(BF)
-        for k in FAR_FIRST:
-            to = (n + k) % NY
-
-            @pl.when(to < 7)
-            def _():
-                send(zbuf.at[b, :, ds(to * 128, 128)], zrecv.at[b, k - 1], psem.at[5 + b], qsem.at[5 + b], here.y_peer(k))
+    for t in last:
+        t.x_back()
+    gram.core_back()
+    yield "gcb"
+    for g in range(CHAINS):
+        last[g].finish()
+        rows = slice(g * M, (g + 1) * M)
+        for b in range(2):
+            i = 2 * g + b
+            zbuf[b, rows, 0:832] = dot_nt(img4[rows], wt2[b]).astype(BF)
+            for k in FAR_FIRST:
+                to = (n + k) % NY
+
+                @pl.when(to < 7)
+                def _():
+                    send(zbuf.at[b, rows, ds(to * 128, 128)], zrecv.at[i, k - 1], zss.at[i], zrs.at[i], here.y_peer(k))
 
     def drain_z():
-        for b in range(2):
+        for i in range(2 * CHAINS):
 
             @pl.when(n < 7)
             def _():
-                wait_bytes(zrecv.at[b, 0:6], psem.at[5 + b])
+                wait_bytes(zrecv.at[i, 0:6], zss.at[i])
 
             @pl.when(n == 7)
             def _():
-                wait_bytes(zrecv.at[b], psem.at[5 + b])
+                wait_bytes(zrecv.at[i], zss.at[i])
 
     drains.append(drain_z)
-    x_ref[...] = gfull[...]
+    gram.finish()
+    g = gram.full
+    x_ref[0:H, 0:H] = g[0, 0:H]
+    x_ref[0:H // 2, H:R] = g[0, H:GROWS]
+    x_ref[H // 2:H, H:R] = g[1, H:GROWS]
+    x_ref[H:R, 0:H] = jnp.zeros((H, H), F32)
+    x_ref[H:R, H:R] = g[1, 0:H]
+    yield "gram"
     factor = inverse_factor(x_ref)
-    for _ in range(5):
+    for _ in range(3):
         next(factor)
 
     @pl.when(n < 7)
     def _():
-        for b in range(2):
-            wait_bytes(zrecv.at[b], qsem.at[5 + b])
-            total = zbuf[b, :, ds(n * 128, 128)].astype(F32)
+        for i in range(2 * CHAINS):
+            wait_bytes(zrecv.at[i], zrs.at[i])
+            rows = slice((i // 2) * M, (i // 2 + 1) * M)
+            total = zbuf[i % 2, rows, ds(n * 128, 128)].astype(F32)
             for k in range(7):
-                total = total + zrecv[b, k].astype(F32)
-            zpair[b] = total.astype(BF)
+                total = total + zrecv[i, k].astype(F32)
+            zpair[i % 2, rows] = total.astype(BF)
         to = zall.at[ds(core * H, H)]
         send(zpair.at[1 - core], to, psem.at[8], qsem.at[8], here.sibling)
         to[...] = zpair[core]
@@ -507,13 +581,14 @@
 
 def on_device(weight, whitening, sketch):
     vmem = pl.BlockSpec(memory_space=pltpu.VMEM)
-    hbm = pl.BlockSpec(memory_space=pl.ANY)
+    hbm = pl.BlockSpec(memory_space=pltpu.HBM)
     vm = pltpu.VMEM
     scratch = []
     for lay in WIDE:
         scratch += wide_scratch(lay)
     for width in NARROW:
         scratch += narrow_scratch(width)
+    scratch += gram_scratch()
     scratch += [
         vm((2, 832, 1024), BF),
         vm((2 * H, 1024), BF),
@@ -525,20 +600,20 @@
         vm((H, 1024), BF),
         vm((H, 1024), BF),
         vm((H, 1024), BF),
-        vm((H, R), F32),
-        vm((R, R), F32),
         vm((H, 2 * H), BF),
         vm((2, H, 832), BF),
         vm((R, 2 * H), BF),
         vm((2 * H, R), F32),
         vm((R, R), F32),
         vm((2, H, 896), BF),
-        vm((2, 7, H, 128), BF),
+        vm((2 * CHAINS, 7, M, 128), BF),
         vm((2, H, 128), BF),
         vm((R, 128), BF),
         vm((R, 128), BF),
         vm((7, 32, 128), BF),
         pltpu.SemaphoreType.DMA((3,)),
+        pltpu.SemaphoreType.DMA((2 * CHAINS,)),
+        pltpu.SemaphoreType.DMA((2 * CHAINS,)),
         pltpu.SemaphoreType.DMA((9,)),
         pltpu.SemaphoreType.DMA((9,)),
     ]
@@ -552,7 +627,7 @@
         out_specs=(vmem, vmem),
         scratch_shapes=scratch,
         compiler_params=pltpu.CompilerParams(
-            collective_id=0, has_side_effects=True, vmem_limit_bytes=48 * 1024 * 1024
+            collective_id=0, has_side_effects=True, vmem_limit_bytes=60 * 1024 * 1024
         ),
         cost_estimate=pl.CostEstimate(flops=2_300_000_000, bytes_accessed=3_000_000, transcendentals=256),
     )(weight.T, whitening, sketch)

time: 156 us -> 147 us (0.942); the launches traced: 153 us -> 147 us
  Pallas kernels: 148 us -> 144 us
  local copies, waits for them, and re-layouts: 4.66 us -> 2.87 us
    pallas_call x1, Pallas kernels: 148 us -> 144 us  [on_device(): pl.pallas_call(kernel, out_shape=(jax.ShapeDtypeStruct((16, R), F32), jax...]
    unnamed x8 -> x2, local copies, waits for them, and re-layouts: 4.66 us -> 2.87 us
where the time goes in v4:
time: 147 us
  Pallas kernels  144 us (98%)
  local copies, waits for them, and re-layouts  2.87 us (2%)
    pallas_call x1, Pallas kernels, on_device(): pl.pallas_call(kernel, out_shape=(jax.ShapeDtypeStruct((16, R), F32), jax...  144 us

profile of v4, /device:TPU:1, one launch (start us, length us, event | category | flops | bytes accessed | tf_op | source)
XLA Modules:
  0.0 147.0 jit_solution(2180808772578258748)
XLA Ops:
  0.6 143.5 %shard_map.50 = (f32[16,256]{1,0:T(8,128)}, f32[32,832]{1,0:T(8,128)}) custom-call(bf16[832,1024]{1,0:T(8,128)(2,1)} %bitcast.1, bf16[128,1024]{1,0:T(8,128)(2,1)} %u_hbm.1, bf16[832,256]{1,0:T(8,128)(2,1)} %s_hbm.1), custom_call_target="tpu_custom_call" | custom-call | flops 2300000000 | bytes 3000000 | tf_op jit(solution)/shard_map/pallas_call | solution.py:620
  144.1 1.3 copy.7
  145.5 1.6 %copy.8 = f32[32,832]{1,0:T(8,128)} copy(f32[32,832]{1,0:T(8,128)} %get-tuple-element.5) | data formatting | bytes 212992

commit v5 on v4

--- a/solution.py
+++ b/solution.py
@@ -12,12 +12,14 @@
 H = 128
 NX, NZ, NY = 4, 8, 8
 CHAINS = 2
-M = H // CHAINS
+XROWS = H // NX
+M = XROWS // CHAINS
 BF = jnp.bfloat16
 F32 = jnp.float32
 MESH = pl.DeviceIdType.MESH
 FAR_FIRST = (4, 3, 5, 2, 6, 1, 7)
-ROUNDS = ("x_step", "z_step", "z_back", "x_back", "finish")
+NEAR = (3, 5, 2, 6, 1, 7)
+ARRIVAL = (0, 1, 3, 2)
 
 
 def ds(start, size):
@@ -59,6 +61,9 @@
     def z_peer(self, k):
         return self.wide((self.z + k) % NZ, self.x, self.core)
 
+    def far_peer(self, k):
+        return self.wide((self.z + NZ // 2) % NZ, (self.x + k) % NX, self.core)
+
     def y_peer(self, k):
         return {"narrow": (self.n + k) % NY}
 
@@ -75,20 +80,19 @@
 
 
 class Cols:
-    dtype = BF
-
-    def __init__(self, base, m):
-        self.base, self.m, self.rows = base, m, m // NX
-        self.xc, self.zc = (m // NX, 1024), (m // NX, 128)
+    dtype, xc, zc = BF, (M, 1024), (M, 128)
+
+    def __init__(self, g):
+        self.base = g * M
 
     def x_of(self, q):
-        return (ds(self.base + q * self.rows, self.rows), slice(None))
+        return (pl.ds(pl.multiple_of(q * XROWS + self.base, M), M), slice(None))
 
     def z_of(self, q):
         return (slice(None), ds(q * 128, 128))
 
     def f_z(self, x, z):
-        return (ds(self.base + x * self.rows, self.rows), ds(z * 128, 128))
+        return (pl.ds(pl.multiple_of(x * XROWS + self.base, M), M), ds(z * 128, 128))
 
 
 def wide_scratch(lay):
@@ -99,30 +103,38 @@
         vm(lay.xc, F32),
         vm(lay.xc, lay.dtype),
         vm((7,) + lay.zc, lay.dtype),
-        pltpu.SemaphoreType.DMA((4,)),
-        pltpu.SemaphoreType.DMA((4,)),
+        vm(lay.zc, lay.dtype),
+        vm((NX,) + lay.zc, lay.dtype),
+        pltpu.SemaphoreType.DMA((7,)),
+        pltpu.SemaphoreType.DMA((13,)),
     ]
 
 
 class WideSum:
     def __init__(self, lay, here, bufs, part, full, extra=None):
         self.lay, self.here, self.part, self.full, self.extra = lay, here, part, full, extra
-        self.xsend, self.xrecv, self.own, self.zsend, self.zrecv, self.ss, self.rs = bufs
-        self.done = 0
+        (self.xsend, self.xrecv, self.own, self.zsend, self.zrecv, self.dsend, self.drecv, self.ss, self.rs) = bufs
+        self.far = (here.z + NZ // 2) % NZ
+
+    def x_part(self, k):
+        lay, here = self.lay, self.here
+        q = lay.x_of((here.x + k) % NX)
+        total = self.part[q]
+        if self.extra is not None:
+            total = total + self.extra[q].astype(F32)
+        if k:
+            self.xsend[k - 1] = total.astype(lay.dtype)
+            send(self.xsend.at[k - 1], self.xrecv.at[k - 1], self.ss.at[0], self.rs.at[0], here.x_peer(k))
+            direct = self.xsend.at[k - 1].at[lay.z_of(self.far)]
+        else:
+            self.own[...] = total
+            self.dsend[...] = self.own[lay.z_of(self.far)].astype(lay.dtype)
+            direct = self.dsend
+        send(direct, self.drecv.at[k], self.ss.at[6], self.rs.at[2], here.far_peer(k))
 
     def x_step(self):
-        lay, here = self.lay, self.here
         for k in (2, 1, 3, 0):
-            q = lay.x_of((here.x + k) % NX)
-            total = self.part[q]
-            if self.extra is not None:
-                total = total + self.extra[q].astype(F32)
-            if k:
-                self.xsend[k - 1] = total.astype(lay.dtype)
-                send(self.xsend.at[k - 1], self.xrecv.at[k - 1], self.ss.at[0], self.rs.at[0], here.x_peer(k))
-            else:
-                self.own[...] = total
-        self.done = 1
+            self.x_part(k)
 
     def z_step(self):
         lay, here = self.lay, self.here
@@ -132,41 +144,56 @@
             total = total + self.xrecv[k].astype(F32)
         self.own[...] = total
         self.zsend[...] = total.astype(lay.dtype)
-        for k in FAR_FIRST:
-            send(self.zsend.at[lay.z_of((here.z + k) % NZ)], self.zrecv.at[k - 1],
+        for i, k in enumerate(NEAR):
+            send(self.zsend.at[lay.z_of((here.z + k) % NZ)], self.zrecv.at[i],
                  self.ss.at[1], self.rs.at[1], here.z_peer(k))
-        self.done = 2
 
     def z_back(self):
         lay, here = self.lay, self.here
-        wait_bytes(self.zrecv, self.rs.at[1])
+        wait_bytes(self.zrecv.at[0:6], self.rs.at[1])
         total = self.own[lay.z_of(here.z)]
-        for k in range(7):
-            total = total + self.zrecv[k].astype(F32)
+        for i in range(6):
+            total = total + self.zrecv[i].astype(F32)
+        wait_bytes(self.drecv, self.rs.at[2])
+        for k in range(NX):
+            total = total + self.drecv[k].astype(F32)
         mine = lay.f_z(here.x, here.z)
         self.full[mine] = total.astype(lay.dtype)
+        mine = self.full.at[mine]
         for k in FAR_FIRST:
-            send(self.full.at[mine], self.full.at[mine], self.ss.at[2], self.rs.at[2], here.z_peer(k))
-        self.done = 3
-
-    def x_back(self):
+            send(mine, mine, self.ss.at[2], self.rs.at[2 + k], here.z_peer(k))
+        self.x_forward(0)
+
+    def x_forward(self, k):
         lay, here = self.lay, self.here
-        wait_bytes(self.zrecv, self.rs.at[2])
-        mine = lay.x_of(here.x)
-        for k in (2, 1, 3):
-            send(self.full.at[mine], self.full.at[mine], self.ss.at[3], self.rs.at[3], here.x_peer(k))
-        self.done = 4
-
-    def finish(self):
-        wait_bytes(self.xrecv, self.rs.at[3])
-        self.done = 5
+        if k:
+            wait_bytes(self.zrecv.at[0], self.rs.at[2 + k])
+        chunk = self.full.at[lay.f_z(here.x, (here.z + NZ - k) % NZ)]
+        for j in (2, 1, 3):
+            send(chunk, chunk, self.ss.at[2 + j], self.rs.at[9 + j], here.x_peer(j))
+
+    def wait_x(self, k):
+        wait_bytes(self.xrecv.at[0], self.rs.at[9 + k])
 
     def drain(self):
-        for i, ref in enumerate((self.xrecv, self.zrecv, self.zrecv, self.xrecv)):
-            if self.done > i:
-                wait_bytes(ref, self.ss.at[i])
-                if self.done == i + 1:
-                    wait_bytes(ref, self.rs.at[i])
+        wait_bytes(self.xrecv, self.ss.at[0])
+        wait_bytes(self.zrecv.at[0:6], self.ss.at[1])
+        wait_bytes(self.zrecv, self.ss.at[2])
+        for k in range(3):
+            wait_bytes(self.xrecv.at[k], self.ss.at[3 + k])
+        wait_bytes(self.drecv, self.ss.at[6])
+
+
+def x_back(chain):
+    for k in (1, 7, 2, 6, 3, 5, 4):
+        for s in chain:
+            s.x_forward(k)
+
+
+def finish(chain):
+    for k in (1, 3, 2):
+        for s in chain:
+            s.wait_x(k)
 
 
 GROWS = 3 * H // 2
@@ -286,6 +313,59 @@
                 wait_bytes(self.recv, self.ss.at[i])
                 if self.done == i + 1:
                     wait_bytes(self.recv, self.rs.at[i])
+
+
+def column_scratch():
+    return [
+        pltpu.VMEM((2, H, 896), BF),
+        pltpu.VMEM((NX, 7, 2, XROWS, 128), BF),
+        pltpu.SemaphoreType.DMA((NX,)),
+        pltpu.SemaphoreType.DMA((NX,)),
+    ]
+
+
+class ColumnSum:
+    def __init__(self, here, bufs):
+        self.here = here
+        self.sendbuf, self.recv, self.ss, self.rs = bufs
+
+    def at(self, k, device):
+        q = (self.here.x + NX - k) % NX
+        return (slice(None), ds(q * XROWS, XROWS), ds(device * 128, 128))
+
+    def product(self, k, image, wt2):
+        here = self.here
+        q = ds(((here.x + NX - k) % NX) * XROWS, XROWS)
+        for b in range(2):
+            self.sendbuf[b, q, 0:832] = dot_nt(image[q], wt2[b]).astype(BF)
+        for j in FAR_FIRST:
+            to = (here.n + j) % NY
+
+            @pl.when(to < 7)
+            def _():
+                send(self.sendbuf.at[self.at(k, to)], self.recv.at[k, j - 1],
+                     self.ss.at[k], self.rs.at[k], here.y_peer(j))
+
+    def total(self, k):
+        wait_bytes(self.recv.at[k], self.rs.at[k])
+        total = self.sendbuf[self.at(k, self.here.n)].astype(F32)
+        for j in range(7):
+            total = total + self.recv[k, j].astype(F32)
+        return total
+
+    def drain(self):
+        for k in range(NX):
+            by_place(self.here, self.recv.at[k], self.ss.at[k])
+
+
+def by_place(here, seven, sem):
+    @pl.when(here.n < 7)
+    def _():
+        wait_bytes(seven.at[0:6], sem)
+
+    @pl.when(here.n == 7)
+    def _():
+        wait_bytes(seven, sem)
 
 
 NB = 64
@@ -349,9 +429,9 @@
         yield b
 
 
-CHAIN = [Cols(g * M, M) for g in range(CHAINS)]
+CHAIN = [Cols(g) for g in range(CHAINS)]
 WIDE = CHAIN * 4
-NARROW = (256, 832, 832, 256)
+NARROW = (256, 256)
 
 
 def body(wt_hbm, u_hbm, s_hbm, basis_ref, proj_ref, scratch, drains):
@@ -364,17 +444,19 @@
         del scratch[:count]
         return got
 
-    wide_bufs = [take(7) for _ in WIDE]
+    wide_bufs = [take(9) for _ in WIDE]
     narrow_bufs = [take(4) for _ in NARROW]
     gram_bufs = take(6)
+    column_bufs = [take(4) for _ in range(2)]
     (wt2, u2, s_ref, csend, crecv, part, img1, img2, img3, img4, v_ref, c2, ya, yb, x_ref,
-     zbuf, zrecv, zpair, zall, pbuf, precv) = take(21)
-    lsem, zss, zrs, psem, qsem = take(5)
+     zpair, zall, pbuf, precv) = take(19)
+    lsem, css, crs, psem, qsem = take(5)
 
     barrier = pltpu.get_barrier_semaphore()
     peers = [here.sibling]
     peers += [here.x_peer(k) for k in range(1, NX)]
     peers += [here.z_peer(k) for k in range(1, NZ)]
+    peers += [here.far_peer(k) for k in range(1, NX)]
     peers += [here.y_peer(k) for k in range(1, NY)]
     for peer in peers:
         pl.semaphore_signal(barrier, inc=1, device_id=peer, device_id_type=MESH)
@@ -385,7 +467,9 @@
     ]
     for load in loads:
         load.start()
-    zbuf[...] = jnp.zeros_like(zbuf)
+    columns = [ColumnSum(here, bufs) for bufs in column_bufs]
+    for c in columns:
+        c.sendbuf[...] = jnp.zeros_like(c.sendbuf)
     for load in loads:
         load.wait()
 
@@ -403,7 +487,6 @@
     drains.append(lambda: wait_bytes(u2.at[0:H], psem.at[2]))
     part[...] = first(core)
     wait_bytes(crecv, qsem.at[0])
-    yield "start"
 
     sums = []
 
@@ -412,45 +495,68 @@
         drains.append(got.drain)
         return got
 
-    def run(chain):
-        for step in ROUNDS:
+    def run(chain, scattered=False):
+        if not scattered:
             for s in chain:
-                getattr(s, step)()
-            yield step
+                s.x_step()
+        for s in chain:
+            s.z_step()
+        for s in chain:
+            s.z_back()
+        x_back(chain)
 
     def narrow(index, full, base=0):
         got = NarrowSum(here, narrow_bufs[index], full, base)
         drains.append(got.drain)
         return got
 
-    yield from run([wide(g, img1, extra=crecv) for g in range(CHAINS)])
+    first_image = [wide(g, img1, extra=crecv) for g in range(CHAINS)]
+    run(first_image)
+    finish(first_image)
     wait_bytes(u2.at[0:H], qsem.at[2])
     n1 = narrow(0, v_ref)
     n1.scatter(dot_nt(img1[...], u2[...]))
-    yield "n1s"
     n1.gather()
-    yield "n1g"
     n1.finish()
     part[...] = dot(v_ref[...], u2[...])
-    yield from run([wide(CHAINS + g, img2) for g in range(CHAINS)])
+    back = [wide(CHAINS + g, img2) for g in range(CHAINS)]
+    run(back)
     wait_bytes(wt2.at[0], qsem.at[1])
-    n2 = [narrow(1 + b, c2.at[b]) for b in range(2)]
-    for b in range(2):
-        n2[b].scatter(dot_nt(img2[...], wt2[b]))
-    yield "n2s"
-    for b in range(2):
-        n2[b].gather()
-    yield "n2g"
-    n2[0].finish()
-    part[...] = dot(c2[0], wt2[0])
-    n2[1].finish()
-    part[...] += dot(c2[1], wt2[1])
-    yield from run([wide(2 * CHAINS + g, img3) for g in range(CHAINS)])
-    n3 = narrow(3, ya, core * H)
+    feature = columns[0]
+    drains.append(feature.drain)
+    for k in ARRIVAL:
+        if k:
+            for s in back:
+                s.wait_x(k)
+        feature.product(k, img2, wt2)
+    for k in ARRIVAL:
+
+        @pl.when(n < 7)
+        def _():
+            mine = feature.at(k, n)
+            c2[mine] = feature.total(k).astype(BF)
+            for j in FAR_FIRST:
+                send(c2.at[mine], c2.at[mine], css.at[k], crs.at[k], here.y_peer(j))
+
+    def drain_c():
+        @pl.when(n < 7)
+        def _():
+            for k in range(NX):
+                wait_bytes(feature.recv.at[k], css.at[k])
+
+    drains.append(drain_c)
+    second = [wide(2 * CHAINS + g, img3) for g in range(CHAINS)]
+    for k in ARRIVAL:
+        by_place(here, feature.recv.at[k], crs.at[k])
+        q = ds(((here.x + NX - k) % NX) * XROWS, XROWS)
+        part[q] = dot(c2[0, q, 0:832], wt2[0]) + dot(c2[1, q, 0:832], wt2[1])
+        for s in second:
+            s.x_part((NX - k) % NX)
+    run(second, scattered=True)
+    finish(second)
+    n3 = narrow(1, ya, core * H)
     n3.scatter(dot_nt(img3[...], u2[...]))
-    yield "n3s"
     n3.gather()
-    yield "n3g"
     n3.finish()
     mine_y = ya.at[ds(core * H, H)]
     send(mine_y, mine_y, psem.at[3], qsem.at[3], here.sibling)
@@ -466,44 +572,21 @@
     gram.part[H:GROWS] = dot_nt(ya[ds(core * (H // 2), H // 2)], ya[H:R])
     gram.z_step()
     yb[...] = ya[...].astype(F32).T
-    yield "gx"
     for t in last:
         t.z_step()
     gram.x_step()
-    yield "gz"
     for t in last:
         t.z_back()
     gram.z_back()
-    yield "gzb"
-    for t in last:
-        t.x_back()
+    x_back(last)
+    z = columns[1]
+    drains.append(z.drain)
+    z.product(0, img4, wt2)
     gram.core_back()
-    yield "gcb"
-    for g in range(CHAINS):
-        last[g].finish()
-        rows = slice(g * M, (g + 1) * M)
-        for b in range(2):
-            i = 2 * g + b
-            zbuf[b, rows, 0:832] = dot_nt(img4[rows], wt2[b]).astype(BF)
-            for k in FAR_FIRST:
-                to = (n + k) % NY
-
-                @pl.when(to < 7)
-                def _():
-                    send(zbuf.at[b, rows, ds(to * 128, 128)], zrecv.at[i, k - 1], zss.at[i], zrs.at[i], here.y_peer(k))
-
-    def drain_z():
-        for i in range(2 * CHAINS):
-
-            @pl.when(n < 7)
-            def _():
-                wait_bytes(zrecv.at[i, 0:6], zss.at[i])
-
-            @pl.when(n == 7)
-            def _():
-                wait_bytes(zrecv.at[i], zss.at[i])
-
-    drains.append(drain_z)
+    for k in ARRIVAL[1:]:
+        for t in last:
+            t.wait_x(k)
+        z.product(k, img4, wt2)
     gram.finish()
     g = gram.full
     x_ref[0:H, 0:H] = g[0, 0:H]
@@ -511,20 +594,15 @@
     x_ref[H // 2:H, H:R] = g[1, H:GROWS]
     x_ref[H:R, 0:H] = jnp.zeros((H, H), F32)
     x_ref[H:R, H:R] = g[1, 0:H]
-    yield "gram"
     factor = inverse_factor(x_ref)
     for _ in range(3):
         next(factor)
 
     @pl.when(n < 7)
     def _():
-        for i in range(2 * CHAINS):
-            wait_bytes(zrecv.at[i], zrs.at[i])
-            rows = slice((i // 2) * M, (i // 2 + 1) * M)
-            total = zbuf[i % 2, rows, ds(n * 128, 128)].astype(F32)
-            for k in range(7):
-                total = total + zrecv[i, k].astype(F32)
-            zpair[i % 2, rows] = total.astype(BF)
+        for k in ARRIVAL:
+            q = ds(((here.x + NX - k) % NX) * XROWS, XROWS)
+            zpair[:, q] = z.total(k).astype(BF)
         to = zall.at[ds(core * H, H)]
         send(zpair.at[1 - core], to, psem.at[8], qsem.at[8], here.sibling)
         to[...] = zpair[core]
@@ -534,7 +612,6 @@
     rr = lax.broadcasted_iota(jnp.int32, (R, R), 0)
     cc = lax.broadcasted_iota(jnp.int32, (R, R), 1)
     inverse = jnp.where(cc <= rr, x_ref[...], 0.0)
-    yield "factor"
     high = inverse.astype(BF)
     low = (inverse - high.astype(F32)).astype(BF)
 
@@ -550,14 +627,7 @@
     basis_ref[...] = lax.dot_general(
         rows, inverse, (((1,), (1,)), ((), ())), preferred_element_type=F32, precision=lax.Precision.HIGHEST
     ) * math.sqrt(D)
-
-    @pl.when(n < 7)
-    def _():
-        wait_bytes(precv.at[0:6], qsem.at[7])
-
-    @pl.when(n == 7)
-    def _():
-        wait_bytes(precv, qsem.at[7])
+    by_place(here, precv, qsem.at[7])
 
     for j in range(6):
         proj_ref[:, j * 128:(j + 1) * 128] = precv[j].astype(F32)
@@ -568,13 +638,10 @@
         wait_bytes(zpair.at[0], psem.at[8])
         wait_bytes(precv, psem.at[7])
 
-    yield "end"
-
 
 def kernel(wt_hbm, u_hbm, s_hbm, basis_ref, proj_ref, *scratch):
     drains = []
-    for _ in body(wt_hbm, u_hbm, s_hbm, basis_ref, proj_ref, scratch, drains):
-        pass
+    body(wt_hbm, u_hbm, s_hbm, basis_ref, proj_ref, scratch, drains)
     for drain in drains:
         drain()
 
@@ -588,7 +655,7 @@
         scratch += wide_scratch(lay)
     for width in NARROW:
         scratch += narrow_scratch(width)
-    scratch += gram_scratch()
+    scratch += gram_scratch() + column_scratch() + column_scratch()
     scratch += [
         vm((2, 832, 1024), BF),
         vm((2 * H, 1024), BF),
@@ -601,19 +668,17 @@
         vm((H, 1024), BF),
         vm((H, 1024), BF),
         vm((H, 2 * H), BF),
-        vm((2, H, 832), BF),
+        vm((2, H, 896), BF),
         vm((R, 2 * H), BF),
         vm((2 * H, R), F32),
         vm((R, R), F32),
-        vm((2, H, 896), BF),
-        vm((2 * CHAINS, 7, M, 128), BF),
         vm((2, H, 128), BF),
         vm((R, 128), BF),
         vm((R, 128), BF),
         vm((7, 32, 128), BF),
         pltpu.SemaphoreType.DMA((3,)),
-        pltpu.SemaphoreType.DMA((2 * CHAINS,)),
-        pltpu.SemaphoreType.DMA((2 * CHAINS,)),
+        pltpu.SemaphoreType.DMA((NX,)),
+        pltpu.SemaphoreType.DMA((NX,)),
         pltpu.SemaphoreType.DMA((9,)),
         pltpu.SemaphoreType.DMA((9,)),
     ]

time: 147 us -> 146 us (level)
  no operation moved by 1% of the time
where the time goes in v5:
time: 146 us
  Pallas kernels  143 us (98%)
  local copies, waits for them, and re-layouts  2.87 us (2%)
    pallas_call x1, Pallas kernels, on_device(): pl.pallas_call(kernel, out_shape=(jax.ShapeDtypeStruct((16, R), F32), jax...  143 us

profile of v5, /device:TPU:1, one launch (start us, length us, event | category | flops | bytes accessed | tf_op | source)
XLA Modules:
  0.0 146.3 jit_solution(15371108562167372876)
XLA Ops:
  0.6 142.8 %shard_map.50 = (f32[16,256]{1,0:T(8,128)}, f32[32,832]{1,0:T(8,128)}) custom-call(bf16[832,1024]{1,0:T(8,128)(2,1)} %bitcast.1, bf16[128,1024]{1,0:T(8,128)(2,1)} %u_hbm.1, bf16[832,256]{1,0:T(8,128)(2,1)} %s_hbm.1), custom_call_target="tpu_custom_call" | custom-call | flops 2300000000 | bytes 3000000 | tf_op jit(solution)/shard_map/pallas_call | solution.py:685
  143.4 1.3 copy.7
  144.7 1.6 %copy.8 = f32[32,832]{1,0:T(8,128)} copy(f32[32,832]{1,0:T(8,128)} %get-tuple-element.5) | data formatting | bytes 212992

commit v6 on v5

--- a/solution.py
+++ b/solution.py
@@ -325,13 +325,30 @@
 
 
 class ColumnSum:
-    def __init__(self, here, bufs):
-        self.here = here
+    def __init__(self, here, bufs, turns):
+        self.here, self.turns = here, turns
         self.sendbuf, self.recv, self.ss, self.rs = bufs
+
+    def tile(self, k, device):
+        if not self.turns:
+            return device
+        q = (self.here.x + NX - k) % NX
+        return (device + NY - 2 * q) % NY
 
     def at(self, k, device):
         q = (self.here.x + NX - k) % NX
-        return (slice(None), ds(q * XROWS, XROWS), ds(device * 128, 128))
+        return (slice(None), ds(q * XROWS, XROWS), ds(self.tile(k, device) * 128, 128))
+
+    def by_place(self, k, seven, sem):
+        tile = self.tile(k, self.here.n)
+
+        @pl.when(tile < 7)
+        def _():
+            wait_bytes(seven.at[0:6], sem)
+
+        @pl.when(tile == 7)
+        def _():
+            wait_bytes(seven, sem)
 
     def product(self, k, image, wt2):
         here = self.here
@@ -341,7 +358,7 @@
         for j in FAR_FIRST:
             to = (here.n + j) % NY
 
-            @pl.when(to < 7)
+            @pl.when(self.tile(k, to) < 7)
             def _():
                 send(self.sendbuf.at[self.at(k, to)], self.recv.at[k, j - 1],
                      self.ss.at[k], self.rs.at[k], here.y_peer(j))
@@ -355,17 +372,7 @@
 
     def drain(self):
         for k in range(NX):
-            by_place(self.here, self.recv.at[k], self.ss.at[k])
-
-
-def by_place(here, seven, sem):
-    @pl.when(here.n < 7)
-    def _():
-        wait_bytes(seven.at[0:6], sem)
-
-    @pl.when(here.n == 7)
-    def _():
-        wait_bytes(seven, sem)
+            self.by_place(k, self.recv.at[k], self.ss.at[k])
 
 
 NB = 64
@@ -467,7 +474,7 @@
     ]
     for load in loads:
         load.start()
-    columns = [ColumnSum(here, bufs) for bufs in column_bufs]
+    columns = [ColumnSum(here, bufs, turns) for bufs, turns in zip(column_bufs, (True, False))]
     for c in columns:
         c.sendbuf[...] = jnp.zeros_like(c.sendbuf)
     for load in loads:
@@ -531,7 +538,7 @@
         feature.product(k, img2, wt2)
     for k in ARRIVAL:
 
-        @pl.when(n < 7)
+        @pl.when(feature.tile(k, n) < 7)
         def _():
             mine = feature.at(k, n)
             c2[mine] = feature.total(k).astype(BF)
@@ -539,15 +546,16 @@
                 send(c2.at[mine], c2.at[mine], css.at[k], crs.at[k], here.y_peer(j))
 
     def drain_c():
-        @pl.when(n < 7)
-        def _():
-            for k in range(NX):
+        for k in range(NX):
+
+            @pl.when(feature.tile(k, n) < 7)
+            def _():
                 wait_bytes(feature.recv.at[k], css.at[k])
 
     drains.append(drain_c)
     second = [wide(2 * CHAINS + g, img3) for g in range(CHAINS)]
     for k in ARRIVAL:
-        by_place(here, feature.recv.at[k], crs.at[k])
+        feature.by_place(k, feature.recv.at[k], crs.at[k])
         q = ds(((here.x + NX - k) % NX) * XROWS, XROWS)
         part[q] = dot(c2[0, q, 0:832], wt2[0]) + dot(c2[1, q, 0:832], wt2[1])
         for s in second:
@@ -627,7 +635,7 @@
     basis_ref[...] = lax.dot_general(
         rows, inverse, (((1,), (1,)), ((), ())), preferred_element_type=F32, precision=lax.Precision.HIGHEST
     ) * math.sqrt(D)
-    by_place(here, precv, qsem.at[7])
+    z.by_place(0, precv, qsem.at[7])
 
     for j in range(6):
         proj_ref[:, j * 128:(j + 1) * 128] = precv[j].astype(F32)

time: 146 us -> 145 us (level)
  no operation moved by 1% of the time
where the time goes in v6:
time: 145 us
  Pallas kernels  142 us (98%)
  local copies, waits for them, and re-layouts  2.87 us (2%)
    pallas_call x1, Pallas kernels, on_device(): pl.pallas_call(kernel, out_shape=(jax.ShapeDtypeStruct((16, R), F32), jax...  142 us

profile of v6, /device:TPU:1, one launch (start us, length us, event | category | flops | bytes accessed | tf_op | source)
XLA Modules:
  0.0 145.1 jit_solution(12713208704057892188)
XLA Ops:
  0.6 141.6 %shard_map.50 = (f32[16,256]{1,0:T(8,128)}, f32[32,832]{1,0:T(8,128)}) custom-call(bf16[832,1024]{1,0:T(8,128)(2,1)} %bitcast.1, bf16[128,1024]{1,0:T(8,128)(2,1)} %u_hbm.1, bf16[832,256]{1,0:T(8,128)(2,1)} %s_hbm.1), custom_call_target="tpu_custom_call" | custom-call | flops 2300000000 | bytes 3000000 | tf_op jit(solution)/shard_map/pallas_call | solution.py:693
  142.2 1.3 copy.7
  143.5 1.6 %copy.8 = f32[32,832]{1,0:T(8,128)} copy(f32[32,832]{1,0:T(8,128)} %get-tuple-element.5) | data formatting | bytes 212992
